TPU v7x, 256 devices: a whole 4x4x8 slice. The times are simulated.
256 devices in a mesh: row: 16 (over z, y_hi), col: 16 (over y_lo, x, core).
Axes of the slice: x: 4, y: 4 (y_hi: 2, y_lo: 2; y = y_hi * 2 + y_lo), z: 8, core: 2. Of those that a mesh axis runs over, the one named last changes fastest.
Arguments:
- acts_panel: bfloat16 [8192, 1024], P('row', 'col')
- acts_trail: bfloat16 [8192, 32768], P('row', 'col')
- weight_panel: float32 [16384, 1024], P('row', 'col'), may hold values from -6 to 6
- block_order: int32 [8], replicated, may hold values from 0 to 7, each once
Outputs:
- slab_factor: float32 [1024, 32768], P('row', 'col')
- pruned_weight: float32 [16384, 1024], P('row', 'col')
Inputs may be any that keep to these rules, and one draw needn't show every extreme that they name: `block_order`: each block number once.
All inputs are finite; a program needn't handle non-finite values.
Results may differ from a plain program's by a relative error of at most 0.0003.
Values may be sent and summed in bfloat16 or wider, within the bound.
No kernel may reach another device: no remote copies, remote signals or barrier semaphores. Data moves between devices by JAX's collectives and lax.ppermute only.
A program may use at most 128 MiB of HBM per device.

v0:
```python
import jax
import jax.numpy as jnp
from jax import lax
from jax.sharding import PartitionSpec as P

PANEL = 1024
NB = 128
NPRUNE = 4


DAMP_SHARE = 0.01


def choose(block_order):
    offsets = jnp.arange(NB, dtype=jnp.int32)
    chosen = (block_order[:NPRUNE, None] * NB + offsets[None, :]).reshape(-1)
    channels = jnp.arange(PANEL, dtype=jnp.int32)
    return (channels[:, None] == chosen[None, :]).astype(jnp.float32)


def factorize(gram_panel):
    mean_diag = jnp.mean(jnp.diagonal(gram_panel))
    identity = jnp.eye(PANEL, dtype=jnp.float32)
    hessian = gram_panel + DAMP_SHARE * mean_diag * identity
    factor = jnp.linalg.cholesky(hessian)
    return lax.linalg.triangular_solve(factor, identity, left_side=True, lower=True)


def on_device(acts_panel, acts_trail, weight_panel, block_order):
    high = lax.Precision.HIGHEST
    n_row = lax.axis_size("row")
    tokens_all = acts_panel.shape[0] * n_row
    panel_dev = acts_panel.shape[1]
    rows_dev = PANEL // n_row
    panel_full = lax.all_gather(acts_panel, "col", axis=1, tiled=True)
    local_strip = jnp.einsum(
        "tp,tq->pq", panel_full, acts_panel, preferred_element_type=jnp.float32
    )
    strip_total = lax.psum(local_strip, "row")
    gram_total = lax.all_gather(strip_total, "col", axis=1, tiled=True)
    inverse_factor = factorize(gram_total / tokens_all)
    slab_rows = (
        lax.psum_scatter(
            jnp.einsum("tp,tq->pq", panel_full, acts_trail, preferred_element_type=jnp.float32),
            "row",
            scatter_dimension=0,
            tiled=True,
        )
        / tokens_all
    )
    own_columns = lax.dynamic_slice_in_dim(
        inverse_factor, lax.axis_index("row") * rows_dev, rows_dev, 1
    )
    slab_factor = lax.psum_scatter(
        jnp.dot(own_columns, slab_rows, precision=high), "row", scatter_dimension=0, tiled=True
    )
    select_full = choose(block_order)
    own_start = lax.axis_index("col") * panel_dev
    inverse_cols = jnp.dot(inverse_factor, select_full, precision=high)
    inverse_block = jnp.dot(inverse_cols.T, inverse_cols, precision=high)
    inverse_own = lax.dynamic_slice_in_dim(inverse_factor, own_start, panel_dev, 1)
    inverse_rows = jnp.dot(inverse_cols.T, inverse_own, precision=high)
    weight_full = lax.all_gather(weight_panel, "col", axis=1, tiled=True)
    pruned_cols = jnp.dot(weight_full, select_full, precision=high)
    block_root = jnp.linalg.cholesky(inverse_block)
    middle = lax.linalg.triangular_solve(block_root, pruned_cols.T, left_side=True, lower=True)
    coefficients = lax.linalg.triangular_solve(
        block_root, middle, left_side=True, lower=True, transpose_a=True
    )
    pruned_weight = weight_panel - jnp.dot(coefficients.T, inverse_rows, precision=high)
    return (slab_factor, pruned_weight)


def solution(mesh):
    return jax.shard_map(
        on_device,
        mesh=mesh,
        in_specs=(P("row", "col"), P("row", "col"), P("row", "col"), P()),
        out_specs=(P("row", "col"), P("row", "col")),
        check_vma=False,
    )
```

profile of v0, /device:TPU:2, one launch (start us, length us, event | category | flops | bytes accessed | tf_op | source)
XLA Modules:
  0.0 897.7 jit_solution(15502902257737704898)
XLA Ops:
  8.0 39.6 %all-gather.4.cloned.1.call-done = bf16[512,1024]{0,1:T(8,128)(2,1)} async-done(((bf16[512,64]{0,1:T(8,128)(2,1)}), bf16[512,1024]{0,1:T(8,128)(2,1)}) %all-gather.4.cloned.1.call-update) | async-done | bytes 1048592 | tf_op jit(solution)/shard_map/all_gather | solution.py:35
  47.5 2.4 fusion.156
  50.0 158.2 %all-reduce.4.cloned.1.call-done = f32[1024,64]{0,1:T(8,128)} async-done(((f32[1024,64]{0,1:T(8,128)}), f32[1024,64]{0,1:T(8,128)}) %all-reduce.4.cloned.1.call-update) | async-done | bytes 262160 | tf_op jit(solution)/shard_map/psum | solution.py:39
  208.3 6.8 fusion.157
  216.1 2.5 fusion.1
  218.5 29.7 %all-gather.6.cloned.1.call-done = f32[1024,1024]{0,1:T(8,128)} async-done(((f32[1024,64]{0,1:T(8,128)}), f32[1024,1024]{0,1:T(8,128)}) %all-gather.6.cloned.1.call-update) | async-done | bytes 4194320 | tf_op jit(solution)/shard_map/all_gather | solution.py:40
  248.2 5.0 broadcast_multiply_fusion
  253.2 17.2 %gather_fusion = f32[1024]{0:T(1024)S(1)} fusion(f32[1024,1024]{0,1:T(8,128)} %broadcast_multiply_fusion, s32[1024]{0:T(1024)S(1)} %bitcast.191), kind=kCustom, calls=%fused_computation | custom fusion | bytes 16384 | tf_op jit(solution)/shard_map/jit(diagonal)/cond/branch_0_fun/gather | solution.py:22
  271.7 5.1 select_add_fusion
  276.7 5.8 copy.24
  282.6 4.6 fusion
  289.1 11.7 %cholesky.277 = f32[128,128]{1,0:T(8,128)S(1)} custom-call(f32[128,128]{1,0:T(8,128)S(1)} %cholesky.726), custom_call_target="Cholesky" | custom-call | tf_op jit(solution)/shard_map/jit(cholesky)/cholesky | solution.py:25
  300.9 9.8 %custom-call.73 = f32[1,128,128]{1,2,0:T(8,128)S(1)} custom-call(f32[1,128,128]{2,1,0:T(8,128)S(1)} %get-tuple-element.97), custom_call_target="InvertDiagBlocksLowerTriangular" | custom-call | tf_op jit(solution)/shard_map/jit(cholesky)/cholesky | solution.py:25
  314.1 11.7 %cholesky.300 = f32[128,128]{1,0:T(8,128)S(1)} custom-call(f32[128,128]{1,0:T(8,128)S(1)} %cholesky.730), custom_call_target="Cholesky" | custom-call | tf_op jit(solution)/shard_map/jit(cholesky)/cholesky | solution.py:25
  326.1 2.5 cholesky.309
  328.6 9.8 %custom-call.74 = f32[1,128,128]{1,2,0:T(8,128)S(1)} custom-call(f32[1,128,128]{2,1,0:T(8,128)S(1)} %get-tuple-element.95), custom_call_target="InvertDiagBlocksLowerTriangular" | custom-call | tf_op jit(solution)/shard_map/jit(cholesky)/cholesky | solution.py:25
  341.1 2.7 convolution_subtract_fusion.10
  343.9 11.7 %cholesky.325 = f32[128,128]{1,0:T(8,128)S(1)} custom-call(f32[128,128]{1,0:T(8,128)S(1)} %cholesky.735), custom_call_target="Cholesky" | custom-call | tf_op jit(solution)/shard_map/jit(cholesky)/cholesky | solution.py:25
  356.4 9.8 %custom-call.75 = f32[1,128,128]{1,2,0:T(8,128)S(1)} custom-call(f32[1,128,128]{2,1,0:T(8,128)S(1)} %get-tuple-element.93), custom_call_target="InvertDiagBlocksLowerTriangular" | custom-call | tf_op jit(solution)/shard_map/jit(cholesky)/cholesky | solution.py:25
  367.4 3.3 convolution_subtract_fusion.11
  370.8 11.7 %cholesky.593 = f32[128,128]{1,0:T(8,128)S(1)} custom-call(f32[128,128]{1,0:T(8,128)S(1)} %cholesky.740), custom_call_target="Cholesky" | custom-call | tf_op jit(solution)/shard_map/jit(cholesky)/cholesky | solution.py:25
  383.3 9.8 %custom-call.76 = f32[1,128,128]{1,2,0:T(8,128)S(1)} custom-call(f32[1,128,128]{2,1,0:T(8,128)S(1)} %get-tuple-element.91), custom_call_target="InvertDiagBlocksLowerTriangular" | custom-call | tf_op jit(solution)/shard_map/jit(cholesky)/cholesky | solution.py:25
  394.2 3.1 convolution_subtract_fusion.12
  397.4 12.1 %cholesky.612 = f32[128,128]{1,0:T(8,128)S(1)} custom-call(f32[128,128]{1,0:T(8,128)S(1)} %cholesky.745), custom_call_target="Cholesky" | custom-call | tf_op jit(solution)/shard_map/jit(cholesky)/cholesky | solution.py:25
  410.3 9.8 %custom-call.84 = f32[1,128,128]{1,2,0:T(8,128)S(1)} custom-call(f32[1,128,128]{2,1,0:T(8,128)S(1)} %get-tuple-element.89), custom_call_target="InvertDiagBlocksLowerTriangular" | custom-call | tf_op jit(solution)/shard_map/jit(cholesky)/cholesky/custom-call.16 | solution.py:25
  421.2 3.1 convolution_subtract_fusion.14
  424.3 11.7 %cholesky.628 = f32[128,128]{1,0:T(8,128)S(1)} custom-call(f32[128,128]{1,0:T(8,128)S(1)} %cholesky.750), custom_call_target="Cholesky" | custom-call | tf_op jit(solution)/shard_map/jit(cholesky)/cholesky | solution.py:25
  436.8 9.8 %custom-call.85 = f32[1,128,128]{1,2,0:T(8,128)S(1)} custom-call(f32[1,128,128]{2,1,0:T(8,128)S(1)} %get-tuple-element.87), custom_call_target="InvertDiagBlocksLowerTriangular" | custom-call | tf_op jit(solution)/shard_map/jit(cholesky)/cholesky/custom-call.17 | solution.py:25
  447.6 2.9 convolution_subtract_fusion.16
  450.4 11.7 %cholesky.644 = f32[128,128]{1,0:T(8,128)S(1)} custom-call(f32[128,128]{1,0:T(8,128)S(1)} %cholesky.755), custom_call_target="Cholesky" | custom-call | tf_op jit(solution)/shard_map/jit(cholesky)/cholesky | solution.py:25
  462.9 9.8 %custom-call.86 = f32[1,128,128]{1,2,0:T(8,128)S(1)} custom-call(f32[1,128,128]{2,1,0:T(8,128)S(1)} %get-tuple-element.85), custom_call_target="InvertDiagBlocksLowerTriangular" | custom-call | tf_op jit(solution)/shard_map/jit(cholesky)/cholesky/custom-call.18 | solution.py:25
  475.7 11.7 %cholesky.658 = f32[128,128]{1,0:T(8,128)S(1)} custom-call(f32[128,128]{1,0:T(8,128)S(1)} %convolution_subtract_fusion.17), custom_call_target="Cholesky" | custom-call | tf_op jit(solution)/shard_map/jit(cholesky)/cholesky | solution.py:25
  497.9 4.8 select_select_fusion
  502.8 28.7 %while.2 = (s32[]{:T(128)}, f32[1024,1024]{0,1:T(8,128)}, s32[8,2]{0,1:T(2,128)S(1)}, f32[8,128,128]{2,1,0:T(8,128)}, s32[]{:T(128)}) while((s32[]{:T(128)}, f32[1024,1024]{0,1:T(8,128)}, s32[8,2]{0,1:T(2,128)S(1)}, f32[8,128,128]{2,1,0:T(8,128)}, s32[]{:T(128)}) %tuple.79), condition=%wide.while_cond, body=%wide.while_body.sunk | while | flops 2 | bytes 393329 | solution.py:26
  503.4 2.3 dynamic-slice.14
  507.0 2.2 dynamic-slice.14
  510.6 2.2 dynamic-slice.14
  514.2 2.2 dynamic-slice.14
  517.8 2.2 dynamic-slice.14
  521.4 2.2 dynamic-slice.14
  531.5 79.8 %custom-call.77 = f32[8,128,128]{1,2,0:T(8,128)S(1)} custom-call(f32[8,128,128]{2,1,0:T(8,128)} %get-tuple-element.12), custom_call_target="InvertDiagBlocksLowerTriangular" | custom-call | tf_op jit(solution)/shard_map/triangular_solve | solution.py:26
  612.6 2.4 convolution_subtract_fusion.8
  616.6 2.7 convolution_subtract_fusion.2
  619.3 2.5 constant_dynamic-update-slice_fusion.15
  621.8 3.6 fusion.44
  627.0 4.4 fusion.47
  633.1 5.4 convolution_subtract_fusion.4
  640.0 6.1 convolution_subtract_fusion.3
  647.6 7.6 convolution_subtract_fusion.7
  656.7 10.0 %fusion.79 = f32[1024,2048]{1,0:T(8,128)} fusion(f32[64,2048]{1,0:T(8,128)} %reduce-scatter.3.cloned.1.call-done, f32[1024,1024]{1,0:T(8,128)} %convolution_dynamic-update-slice_fusion, s32[]{:T(128)S(6)} %select_n.19), kind=kOutput, calls=%fused_computation.113 | convolution fusion | flops 1610743808 | bytes 9437188 | tf_op jit(solution)/shard_map/dot_general | solution.py:55
  667.5 7.2 fusion.18
  674.6 5.7 fusion.19
  680.3 3.5 fusion.158
  687.6 11.7 %cholesky.671 = f32[128,128]{1,0:T(8,128)S(1)} custom-call(f32[128,128]{1,0:T(8,128)S(1)} %cholesky.759), custom_call_target="Cholesky" | custom-call | tf_op jit(solution)/shard_map/jit(cholesky)/cholesky | solution.py:65
  699.5 9.8 %custom-call.87 = f32[1,128,128]{1,2,0:T(8,128)S(1)} custom-call(f32[1,128,128]{2,1,0:T(8,128)S(1)} %get-tuple-element.83), custom_call_target="InvertDiagBlocksLowerTriangular" | custom-call | tf_op jit(solution)/shard_map/jit(cholesky)/cholesky/custom-call.16 | solution.py:65
  711.8 12.1 %cholesky.682 = f32[128,128]{1,0:T(8,128)S(1)} custom-call(f32[128,128]{1,0:T(8,128)S(1)} %cholesky.763), custom_call_target="Cholesky" | custom-call | tf_op jit(solution)/shard_map/jit(cholesky)/cholesky | solution.py:65
  724.0 9.8 %custom-call.88 = f32[1,128,128]{1,2,0:T(8,128)S(1)} custom-call(f32[1,128,128]{2,1,0:T(8,128)S(1)} %get-tuple-element.80), custom_call_target="InvertDiagBlocksLowerTriangular" | custom-call | tf_op jit(solution)/shard_map/jit(cholesky)/cholesky/custom-call.17 | solution.py:65
  735.4 11.7 %cholesky.699 = f32[128,128]{1,0:T(8,128)S(1)} custom-call(f32[128,128]{1,0:T(8,128)S(1)} %cholesky.768), custom_call_target="Cholesky" | custom-call | tf_op jit(solution)/shard_map/jit(cholesky)/cholesky | solution.py:65
  747.1 9.8 %custom-call.89 = f32[1,128,128]{1,2,0:T(8,128)S(1)} custom-call(f32[1,128,128]{2,1,0:T(8,128)S(1)} %get-tuple-element.77), custom_call_target="InvertDiagBlocksLowerTriangular" | custom-call | tf_op jit(solution)/shard_map/jit(cholesky)/cholesky/custom-call.18 | solution.py:65
  758.4 11.7 %cholesky.712 = f32[128,128]{1,0:T(8,128)S(1)} custom-call(f32[128,128]{1,0:T(8,128)S(1)} %convolution_subtract_fusion.18), custom_call_target="Cholesky" | custom-call | tf_op jit(solution)/shard_map/jit(cholesky)/cholesky | solution.py:65
  775.5 10.4 %while.3 = (s32[]{:T(128)}, f32[512,512]{1,0:T(8,128)S(1)}, s32[4,2]{0,1:T(2,128)S(1)}, f32[4,128,128]{2,1,0:T(8,128)}, s32[]{:T(128)}) while((s32[]{:T(128)}, f32[512,512]{1,0:T(8,128)S(1)}, s32[4,2]{0,1:T(2,128)S(1)}, f32[4,128,128]{2,1,0:T(8,128)}, s32[]{:T(128)}) %tuple.82), condition=%wide.while_cond.1, body=%wide.while_body.1.sunk | while | flops 2 | bytes 132205 | solution.py:67
  785.9 40.3 %custom-call.78 = f32[4,128,128]{1,2,0:T(8,128)S(1)} custom-call(f32[4,128,128]{2,1,0:T(8,128)} %get-tuple-element.20), custom_call_target="InvertDiagBlocksLowerTriangular" | custom-call | tf_op jit(solution)/shard_map/triangular_solve | solution.py:67
  840.3 4.6 fusion.77
  847.1 43.5 %reduce-scatter.5.cloned.1.call-done = f32[64,2048]{1,0:T(8,128)} async-done(((f32[1024,2048]{1,0:T(8,128)}), f32[64,2048]{1,0:T(8,128)}) %reduce-scatter.5.cloned.1.call-update) | async-done | bytes 524304 | tf_op jit(solution)/shard_map/reduce_scatter | solution.py:54
  (184 shorter events, 93.0 us)
Async XLA Ops:
  7.2 201.1 %copy-start = (bf16[512,2048]{1,0:T(8,128)(2,1)S(1)}, bf16[512,2048]{1,0:T(8,128)(2,1)}, u32[]{:S(2)}) copy-start(bf16[512,2048]{1,0:T(8,128)(2,1)} %param.11) | copy-start | bytes 6291460
  7.2 40.3 %all-gather.4.cloned.1.call-start = ((), (), s32[]{:S(2)}) async-start(), calls=%async_computation.2 | async-start | bytes 1114112 | tf_op jit(solution)/shard_map/all_gather | solution.py:35
  7.9 200.3 %all-reduce.4.cloned.1.call-start = ((), (), s32[]{:S(2)}) async-start(), calls=%async_computation.3 | async-start | bytes 524288 | tf_op jit(solution)/shard_map/psum | solution.py:39
  49.9 198.3 %all-gather.6.cloned.1.call-start = ((), (), s32[]{:S(2)}) async-start(), calls=%async_computation.4 | async-start | bytes 4456448 | tf_op jit(solution)/shard_map/all_gather | solution.py:40
  208.2 448.5 %reduce-scatter.3.cloned.1.call-start = ((), (), s32[]{:S(2)}) async-start(), calls=%async_computation.5 | async-start | bytes 8912896 | tf_op jit(solution)/shard_map/reduce_scatter | solution.py:43
  215.1 452.4 %all-gather.8.cloned.1.call-start = ((), (), s32[]{:S(2)}) async-start(), calls=%async_computation.7 | async-start | bytes 4456448 | tf_op jit(solution)/shard_map/all_gather | solution.py:63
  215.7 675.0 %reduce-scatter.5.cloned.1.call-start = ((), (), s32[]{:S(2)}) async-start(), calls=%async_computation.6 | async-start | bytes 8912896 | tf_op jit(solution)/shard_map/reduce_scatter | solution.py:54
  287.1 1.9 copy-start.5
  611.3 8.0 copy-start.7
  611.3 5.3 copy-start.4
  619.3 6.1 copy-start.8
  666.7 0.7 copy-start.10
  680.3 6.3 copy-start.2
  686.6 1.0 copy-start.6
  836.6 3.6 copy-start.3
  837.9 7.0 copy-start.9
  838.5 52.1 %copy-start.1 = (bf16[512,2048]{1,0:T(8,128)(2,1)S(1)}, bf16[512,2048]{1,0:T(8,128)(2,1)}, u32[]{:S(2)}) copy-start(bf16[512,2048]{1,0:T(8,128)(2,1)} %param.11) | copy-start | bytes 6291460
Sparse Core Ops, SparseCore 0:
  9.9 37.6 all-gather.3
  50.7 157.4 all-reduce.3
  210.2 37.9 all-gather.5
  252.7 224.0 reduce-scatter.2
  478.7 37.9 all-gather.7
  666.9 223.7 reduce-scatter.4
where the time goes:
time: 904 us; the launch traced here: 898 us
  other arithmetic  392 us (43%)
  waiting for transfers between devices  272 us (30%)
  matrix products  134 us (15%)
  local copies, waits for them, and re-layouts  76 us (8%)
  between operations  23.2 us (3%)
    another operation x30, other arithmetic, factorize(): factor = jnp.linalg.cholesky(hessian)  168 us
    psum x1, waiting for transfers between devices, on_device(): strip_total = lax.psum(local_strip, 'row')  158 us
    another operation x3, other arithmetic, factorize(): lax.linalg.triangular_solve(factor, identity, left_side=True, lower=True)  84.7 us
    another operation x15, other arithmetic, on_device(): block_root = jnp.linalg.cholesky(inverse_block)  79.5 us
    another operation x15, matrix products, factorize(): lax.linalg.triangular_solve(factor, identity, left_side=True, lower=True)  45.3 us
    reduce_scatter x1, waiting for transfers between devices, on_device(): lax.psum_scatter(jnp.dot(own_columns, slab_rows, precision=high), 'row',...  43.5 us
    another operation x3, other arithmetic, on_device(): lax.linalg.triangular_solve(block_root, middle, left_side=True, lower=Tru...  40.4 us
    all_gather x1, waiting for transfers between devices, on_device(): panel_full = lax.all_gather(acts_panel, 'col', axis=1, tiled=True)  39.6 us
  transfers between devices with their start and end apart: 6, of which 4 were waited for; matrix products, arithmetic and copies ran while one was open for 66% of the time, Pallas kernels for 0%

commit v1 on v0

v1 whole, which is shorter than its diff:
```python
import functools

import jax
import jax.numpy as jnp
from jax import lax
from jax.experimental import pallas as pl
from jax.experimental.pallas import tpu as pltpu
from jax.sharding import PartitionSpec as P

f32 = jnp.float32
NB = 128
HIGH = lax.Precision.HIGHEST

def lanes(x):
    return jnp.broadcast_to(x, (8, NB))

def factor_blocks(blocks):
    lane = lax.broadcasted_iota(jnp.int32, (8, NB), 1)
    sub = lax.broadcasted_iota(jnp.int32, (8, NB), 0)
    at = [sub == k for k in range(8)]
    outs = [[] for _ in blocks]
    for j in range(16):
        lo = 8 * j
        inside = (lane >= lo) & (lane < lo + 8)
        unit = jnp.where(lane - lo == sub, 1.0, 0.0).astype(f32)
        for b, rows in enumerate(blocks):
            R = rows[j]
            D = [lanes(R[:, lo + k:lo + k + 1]) for k in range(8)]
            R = jnp.where(inside, unit, R)
            out = jnp.zeros((8, NB), f32)
            for k in range(8):
                p = lanes(D[k][k:k + 1, :])
                inv = 1.0 / p
                bR = lanes(R[k:k + 1, :])
                out = jnp.where(at[k], bR * lax.rsqrt(p), out)
                f = D[k] * inv
                R = jnp.where(at[k], bR * inv, R - f * bR)
                for m in range(k + 1, 8):
                    bD = lanes(D[m][k:k + 1, :])
                    D[m] = jnp.where(at[k], bD * inv, D[m] - f * bD)
            outs[b].append(jnp.where(lane <= lo + sub, out, 0.0))
            if j < 15:
                W = [lanes(R[k:k + 1, :]) for k in range(8)]
                for i in range(j + 1, 16):
                    T = rows[i]
                    acc = lanes(T[:, lo:lo + 1]) * W[0]
                    for k in range(1, 8):
                        acc += lanes(T[:, lo + k:lo + k + 1]) * W[k]
                    rows[i] = jnp.where(inside, 0.0, T) - acc
    return outs

def load_block(ref, k):
    o = pl.multiple_of(k * NB, NB)
    return [ref[pl.ds(pl.multiple_of(o + 8 * i, 8), 8), pl.ds(o, NB)] for i in range(16)]

def eliminate(ref, inv_ref, k, n):
    o = pl.multiple_of(k * NB, NB)
    eye = jnp.where(lax.broadcasted_iota(jnp.int32, (NB, NB), 0) == lax.broadcasted_iota(jnp.int32, (NB, NB), 1), 1.0, 0.0).astype(f32)
    ref[pl.ds(o, NB), pl.ds(o, NB)] = eye
    U = jnp.dot(inv_ref[...], ref[pl.ds(o, NB), :], precision=HIGH, preferred_element_type=f32)
    ref[pl.ds(o, NB), :] = U

    def below(i, _):
        w = pl.multiple_of(i * NB, NB)
        Ui = ref[pl.ds(o, NB), pl.ds(w, NB)]
        ref[pl.ds(w, NB), pl.ds(o, NB)] = jnp.zeros((NB, NB), f32)
        ref[pl.ds(w, NB), :] -= lax.dot_general(Ui, ref[pl.ds(o, NB), :], (((0,), (0,)), ((), ())), precision=HIGH, preferred_element_type=f32)
        return 0
    lax.fori_loop(k + 1, n, below, 0)

def kernel(tokens, order_ref, own_ref, g_ref, x_ref, m_ref, at, inv1, inv2, hst):
    r = lax.broadcasted_iota(jnp.int32, (NB, NB), 0)
    c = lax.broadcasted_iota(jnp.int32, (NB, NB), 1)
    diag = r == c
    tot = jnp.zeros((NB, NB), f32)
    for b in range(8):
        tot += jnp.where(diag, g_ref[b * NB:(b + 1) * NB, b * NB:(b + 1) * NB], 0.0)
    damp = jnp.sum(tot) * (0.01 / 1024.0 / tokens)
    x_ref[...] = g_ref[...] * (1.0 / tokens)
    for b in range(8):
        s = slice(b * NB, (b + 1) * NB)
        x_ref[s, s] += jnp.where(diag, damp, 0.0)
    for a in range(4):
        oa = pl.multiple_of(order_ref[4 + a] * NB, NB)
        os = pl.multiple_of(order_ref[a] * NB, NB)
        for b in range(4):
            ob = pl.multiple_of(order_ref[4 + b] * NB, NB)
            at[a * NB:(a + 1) * NB, b * NB:(b + 1) * NB] = x_ref[pl.ds(oa, NB), pl.ds(ob, NB)]
            hst[a * NB:(a + 1) * NB, b * NB:(b + 1) * NB] = x_ref[pl.ds(os, NB), pl.ds(ob, NB)]

    def both(k, _):
        o1, o2 = factor_blocks([load_block(x_ref, k), load_block(at, k)])
        for i in range(16):
            inv1[8 * i:8 * i + 8, :] = o1[i]
            inv2[8 * i:8 * i + 8, :] = o2[i]
        eliminate(x_ref, inv1, k, 8)
        eliminate(at, inv2, k, 4)
        return 0
    lax.fori_loop(0, 4, both, 0)

    def single(k, _):
        o1, = factor_blocks([load_block(x_ref, k)])
        for i in range(16):
            inv1[8 * i:8 * i + 8, :] = o1[i]
        eliminate(x_ref, inv1, k, 8)
        return 0
    lax.fori_loop(4, 8, single, 0)
    for k in range(7):
        x_ref[k * NB:(k + 1) * NB, (k + 1) * NB:] = jnp.zeros((NB, (7 - k) * NB), f32)
    for k in range(3):
        at[k * NB:(k + 1) * NB, (k + 1) * NB:] = jnp.zeros((NB, (3 - k) * NB), f32)
    own = own_ref[0]
    m_ref[...] = jnp.zeros((512, NB), f32)
    for a in range(4):
        @pl.when(order_ref[a] == own)
        def _():
            m_ref[a * NB:(a + 1) * NB, :] = jnp.where(diag, 1.0, 0.0)
        @pl.when(order_ref[4 + a] == own)
        def _():
            z = lax.dot_general(at[...], at[:, a * NB:(a + 1) * NB], (((0,), (0,)), ((), ())), precision=HIGH, preferred_element_type=f32)
            m_ref[...] = -jnp.dot(hst[...], z, precision=HIGH, preferred_element_type=f32)

def factor_call(gram, order, own, tokens):
    return pl.pallas_call(
        functools.partial(kernel, tokens),
        out_shape=(jax.ShapeDtypeStruct((1024, 1024), f32), jax.ShapeDtypeStruct((512, NB), f32)),
        in_specs=[pl.BlockSpec(memory_space=pltpu.SMEM), pl.BlockSpec(memory_space=pltpu.SMEM), pl.BlockSpec(memory_space=pltpu.VMEM)],
        out_specs=(pl.BlockSpec(memory_space=pltpu.VMEM), pl.BlockSpec(memory_space=pltpu.VMEM)),
        scratch_shapes=[pltpu.VMEM((512, 512), f32), pltpu.VMEM((NB, NB), f32), pltpu.VMEM((NB, NB), f32), pltpu.VMEM((512, 512), f32)],
        compiler_params=pltpu.CompilerParams(vmem_limit_bytes=40 * 1024 * 1024),
    )(order, own, gram)


def slab_kernel(panel_ref, trail_ref, out_ref):
    @pl.when(pl.program_id(0) == 0)
    def _():
        out_ref[...] = jnp.zeros_like(out_ref)

    out_ref[...] += jnp.dot(panel_ref[0], trail_ref[0], preferred_element_type=f32)


def slab_call(panel, trail):
    groups, channels, span = panel.shape
    columns = trail.shape[2]
    return pl.pallas_call(
        slab_kernel,
        grid=(groups,),
        in_specs=[
            pl.BlockSpec((1, channels, span), lambda i: (i, 0, 0)),
            pl.BlockSpec((1, span, columns), lambda i: (i, 0, 0)),
        ],
        out_specs=pl.BlockSpec((channels, columns), lambda i: (0, 0)),
        out_shape=jax.ShapeDtypeStruct((channels, columns), f32),
    )(panel, trail)


def spread(x, axis):
    n = lax.axis_size(axis)
    return lax.all_to_all(jnp.broadcast_to(x[None], (n,) + x.shape), axis, 0, 0)


def on_device(acts_panel, acts_trail, weight_panel, block_order):
    n_row = lax.axis_size("row")
    span, own_n = acts_panel.shape
    tokens = span * n_row
    own_t = acts_panel.T
    everything = lax.all_gather(own_t, ("row", "col"))
    panel_t = spread(own_t, "col").reshape(-1, span)
    strip = lax.dot_general(own_t, panel_t, (((1,), (1,)), ((), ())), preferred_element_type=f32)
    pieces = strip.reshape(8, 8, 2, 512).transpose(0, 2, 1, 3).reshape(16, 8, 512)
    piece = lax.all_to_all(pieces, "row", 0, 0).sum(0)
    strip_total = spread(piece, "row").reshape(8, 2, 8, 512).transpose(0, 2, 1, 3).reshape(64, 1024)
    trail_in, strip_total = lax.optimization_barrier((acts_trail, strip_total))
    gram = spread(strip_total, "col").reshape(1024, 1024)
    trail = lax.all_to_all(trail_in.reshape(span, n_row, -1), "row", 1, 0)
    weight_t = weight_panel.T
    weight_in, gram = lax.optimization_barrier((weight_t, gram))
    weight_all = spread(weight_in, "col").reshape(1024, -1)
    own = lax.axis_index("col")
    inverse_factor, mixing = factor_call(gram, block_order, (own // 2).reshape(1), tokens)
    everything, inverse_factor = lax.optimization_barrier((everything, inverse_factor))
    slab = slab_call(everything.reshape(n_row, 1024, span), trail) * (1.0 / tokens)
    solved = jnp.dot(inverse_factor, slab, precision=HIGH)
    slab_rows = lax.all_to_all(solved.reshape(n_row, 1024 // n_row, -1), "row", 0, 0)
    slab_factor = slab_rows.transpose(1, 0, 2).reshape(1024 // n_row, -1)
    pruned = jnp.concatenate(
        [lax.dynamic_slice_in_dim(weight_all, block_order[q] * NB, NB, 0) for q in range(4)], 0
    )
    own_mixing = lax.dynamic_slice_in_dim(mixing, (own % 2) * own_n, own_n, 1)
    change = lax.dot_general(own_mixing, pruned, (((0,), (0,)), ((), ())), precision=HIGH)
    return (slab_factor, (weight_t - change).T)


def solution(mesh):
    return jax.shard_map(
        on_device,
        mesh=mesh,
        in_specs=(P("row", "col"), P("row", "col"), P("row", "col"), P()),
        out_specs=(P("row", "col"), P("row", "col")),
        check_vma=False,
    )
```

time: 904 us -> 349 us (0.39)
  other arithmetic: 392 us -> 0.02 us
  waiting for transfers between devices: 272 us -> 133 us
  matrix products: 134 us -> 9.18 us
  Pallas kernels: 0 us -> 87.6 us
  blocking collectives: 0 us -> 61 us
  local copies, waits for them, and re-layouts: 76 us -> 16.4 us
  starting transfers between devices: 0.24 us -> 20.1 us
    another operation x51 -> x0, other arithmetic: 372 us -> none  [the longest x30 168 us: factorize(): factor = jnp.linalg.cholesky(hessian)]
    psum x1 -> x0, waiting for transfers between devices: 158 us -> none  [on_device(): strip_total = lax.psum(local_strip, 'row')]
    all_to_all x0 -> x4, waiting for transfers between devices: none -> 133 us  [the longest x2 65.2 us: spread(): return lax.all_to_all(jnp.broadcast_to(x[None], (n,) + x.shape), axis, 0, 0)]
    another operation x49 -> x0, matrix products: 91.6 us -> none  [the longest x15 45.3 us: factorize(): lax.linalg.triangular_solve(factor, identity, left_side=True, lower=True)]
    pallas_call x0 -> x2, Pallas kernels: none -> 87.6 us  [the longest x1 72.4 us: factor_call(): pl.pallas_call(functools.partial(kernel, tokens), out_shape=(jax.ShapeDty...]
    all_gather x3 -> x1, waiting for transfers between devices: 69.2 us -> 0.01 us  [on_device(): everything = lax.all_gather(own_t, ('row', 'col'))]
    all_to_all x0 -> x3, blocking collectives: none -> 61 us  [the longest x2 35.6 us: spread(): return lax.all_to_all(jnp.broadcast_to(x[None], (n,) + x.shape), axis, 0, 0)]
    another operation x83 -> x1, local copies, waits for them, and re-layouts: 48.1 us -> 2.41 us  [on_device(): trail = lax.all_to_all(trail_in.reshape(span, n_row, -1), 'row', 1, 0)]
  transfers between devices with their start and end apart: 6 -> 5, of which waited for: 4 -> 3; matrix products, arithmetic and copies ran while one was open for 66% -> 7% of each run, Pallas kernels for 0% -> 25%
where the time goes in v1:
time: 349 us; the launch traced here: 344 us
  waiting for transfers between devices  133 us (38%)
  Pallas kernels  87.6 us (25%)
  blocking collectives  61 us (17%)
  starting transfers between devices  20.1 us (6%)
  between operations  16.6 us (5%)
  local copies, waits for them, and re-layouts  16.4 us (5%)
  matrix products  9.18 us (3%)
    pallas_call x1, Pallas kernels, factor_call(): pl.pallas_call(functools.partial(kernel, tokens), out_shape=(jax.ShapeDty...  72.4 us
    all_to_all x2, waiting for transfers between devices, spread(): return lax.all_to_all(jnp.broadcast_to(x[None], (n,) + x.shape), axis, 0, 0)  65.2 us
    all_to_all x1, waiting for transfers between devices, on_device(): trail = lax.all_to_all(trail_in.reshape(span, n_row, -1), 'row', 1, 0)  55 us
    all_to_all x2, blocking collectives, spread(): return lax.all_to_all(jnp.broadcast_to(x[None], (n,) + x.shape), axis, 0, 0)  35.6 us
    all_to_all x1, blocking collectives, on_device(): piece = lax.all_to_all(pieces, 'row', 0, 0).sum(0)  25.5 us
    pallas_call x1, Pallas kernels, slab_call(): pl.pallas_call(slab_kernel, grid=(groups,), in_specs=[pl.BlockSpec((1, ch...  15.2 us
    all_to_all x1, waiting for transfers between devices, on_device(): lax.all_to_all(solved.reshape(n_row, 1024 // n_row, -1), 'row', 0, 0)  12.4 us
    all_to_all x2, starting transfers between devices, spread(): return lax.all_to_all(jnp.broadcast_to(x[None], (n,) + x.shape), axis, 0, 0)  9.98 us
  transfers between devices with their start and end apart: 5, of which 3 were waited for; matrix products, arithmetic and copies ran while one was open for 7% of the time, Pallas kernels for 25%

profile of v1, /device:TPU:2, one launch (start us, length us, event | category | flops | bytes accessed | tf_op | source)
XLA Modules:
  0.0 344.4 jit_solution(10310457360673941632)
XLA Ops:
  7.2 0.0 copy-start.3
  7.2 0.0 all-gather.3.cloned.1.call-start
  7.2 0.7 all-gather.3.cloned.1.call-update
  7.9 0.9 broadcast_in_dim.8
  8.8 19.0 %all_to_all.45 = bf16[16,64,512]{2,1,0:T(8,128)(2,1)S(1)} all-to-all(bf16[16,64,512]{2,1,0:T(8,128)(2,1)S(1)} %broadcast_in_dim.8), channel_id=1, replica_groups=mesh['row'=16,'col'=16] {'col'}, dimensions={0} | all-to-all | bytes 2097152 | tf_op jit(solution)/shard_map/all_to_all | solution.py:159
  27.8 0.0 copy-done.3
  27.8 0.4 fusion.15
  28.3 25.5 %all_to_all.46 = f32[16,8,512]{2,1,0:T(8,128)S(1)} all-to-all(f32[16,8,512]{2,1,0:T(8,128)S(1)} %bitcast.50), channel_id=1, replica_groups=mesh['row'=16,'col'=16] {'row'}, dimensions={0} | all-to-all | bytes 524288 | tf_op jit(solution)/shard_map/all_to_all | solution.py:171
  53.8 16.6 %all_to_all.47 = f32[16,8,512]{2,1,0:T(8,128)S(1)} all-to-all(f32[16,8,512]{2,1,0:T(8,128)S(1)} %broadcast_in_dim.9), channel_id=1, replica_groups=mesh['row'=16,'col'=16] {'row'}, dimensions={0} | all-to-all | bytes 524288 | tf_op jit(solution)/shard_map/all_to_all | solution.py:159
  70.4 2.5 broadcast_in_dim.10
  72.9 4.9 %all-to-all-start.3 = ((f32[16,64,1024]{2,1,0:T(8,128)}), f32[16,64,1024]{2,1,0:T(8,128)}, u32[]{:S(2)}, u32[]{:S(2)}) async-start(f32[16,64,1024]{2,1,0:T(8,128)} %broadcast_in_dim.10), calls=%async_computation.3 | async-start | bytes 8388608 | tf_op jit(solution)/shard_map/all_to_all | solution.py:159
  77.7 2.9 copy.10
  80.7 2.4 copy.11
  83.1 0.0 copy-start.4
  83.1 65.2 %all-to-all-done.3 = f32[16,64,1024]{2,1,0:T(8,128)} async-done(((f32[16,64,1024]{2,1,0:T(8,128)}), f32[16,64,1024]{2,1,0:T(8,128)}, u32[]{:S(2)}, u32[]{:S(2)}) %all-to-all-start.3) | async-done | bytes 4194336 | tf_op jit(solution)/shard_map/all_to_all | solution.py:159
  148.3 3.7 %all-to-all-start.4 = ((bf16[1,512,16,128]{3,1,0,2:T(8,128)(2,1)}), bf16[1,512,16,128]{3,1,0,2:T(8,128)(2,1)S(1)}, u32[]{:S(2)}, u32[]{:S(2)}) async-start(bf16[1,512,16,128]{3,1,0,2:T(8,128)(2,1)} %copy.11), calls=%async_computation.4 | async-start | bytes 4194304 | tf_op jit(solution)/shard_map/all_to_all | solution.py:175
  152.0 55.0 %all-to-all-done.4 = bf16[1,512,16,128]{3,1,0,2:T(8,128)(2,1)S(1)} async-done(((bf16[1,512,16,128]{3,1,0,2:T(8,128)(2,1)}), bf16[1,512,16,128]{3,1,0,2:T(8,128)(2,1)S(1)}, u32[]{:S(2)}, u32[]{:S(2)}) %all-to-all-start.4) | async-done | bytes 2097184 | tf_op jit(solution)/shard_map/all_to_all | solution.py:175
  207.0 0.0 copy-done.4
  207.0 0.0 copy-start.2
  207.0 2.6 broadcast_in_dim.11
  209.6 0.0 copy-done.2
  209.6 0.0 copy-start.1
  209.6 5.1 %all-to-all-start.6 = ((f32[16,64,1024]{2,1,0:T(8,128)}), f32[16,64,1024]{2,1,0:T(8,128)}, u32[]{:S(2)}, u32[]{:S(2)}) async-start(f32[16,64,1024]{2,1,0:T(8,128)} %broadcast_in_dim.11), calls=%async_computation.6 | async-start | bytes 8388608 | tf_op jit(solution)/shard_map/all_to_all | solution.py:159
  214.7 0.0 copy-done.1
  214.7 72.4 %shard_map.59 = (f32[1024,1024]{1,0:T(8,128)S(1)}, f32[512,128]{1,0:T(8,128)S(1)}) custom-call(s32[8]{0:T(128)S(1)} %copy-done.1, s32[1]{0:T(128)} %bitcast.2.own_ref, f32[1024,1024]{1,0:T(8,128)} %bitcast.14.g_ref), custom_call_target="tpu_custom_call" | custom-call | tf_op jit(solution)/shard_map/pallas_call | solution.py:124
  287.2 0.0 copy-start
  287.2 2.0 copy-done
  289.1 0.0 all-gather.3.cloned.1.call-done
  289.1 15.2 %shard_map.60 = f32[1024,128]{1,0:T(8,128)} custom-call(bf16[16,1024,512]{2,1,0:T(8,128)(2,1)} %bitcast.45, bf16[16,512,128]{2,1,0:T(8,128)(2,1)} %bitcast.46), custom_call_target="tpu_custom_call" | custom-call | tf_op jit(solution)/shard_map/pallas_call | solution.py:145
  304.3 6.5 %fusion.11 = f32[1024,128]{1,0:T(8,128)} fusion(f32[1024,1024]{1,0:T(8,128)} %copy-done, f32[1024,128]{1,0:T(8,128)} %shard_map.60), kind=kOutput, calls=%fused_computation.10 | convolution fusion | flops 1610743808 | bytes 5242880 | tf_op jit(solution)/shard_map/dot_general | solution.py:183
  310.9 0.0 all-to-all-done.6
  310.9 6.4 %all-to-all-start.5 = ((f32[16,64,128]{2,1,0:T(8,128)}), f32[16,64,128]{2,1,0:T(8,128)S(1)}, u32[]{:S(2)}, u32[]{:S(2)}) async-start(f32[16,64,128]{2,1,0:T(8,128)} %bitcast.20), calls=%async_computation.5 | async-start | bytes 1048576 | tf_op jit(solution)/shard_map/all_to_all | solution.py:184
  317.3 0.6 fusion.20
  320.4 1.7 constant_dynamic-slice_fusion.3
  322.1 2.2 fusion.8
  324.3 12.4 %all-to-all-done.5 = f32[16,64,128]{2,1,0:T(8,128)S(1)} async-done(((f32[16,64,128]{2,1,0:T(8,128)}), f32[16,64,128]{2,1,0:T(8,128)S(1)}, u32[]{:S(2)}, u32[]{:S(2)}) %all-to-all-start.5) | async-done | bytes 524320 | tf_op jit(solution)/shard_map/all_to_all | solution.py:184
  336.7 0.8 copy_bitcast_fusion
  (2 shorter events, 0.0 us)
Async XLA Ops:
  7.2 20.7 %copy-start.3 = (bf16[512,64]{0,1:T(8,128)(2,1)S(1)}, bf16[512,64]{0,1:T(8,128)(2,1)}, u32[]{:S(2)}) copy-start(bf16[512,64]{0,1:T(8,128)(2,1)} %param.4) | copy-start | bytes 196612
  7.2 282.0 %all-gather.3.cloned.1.call-start = ((), (), s32[]{:S(2)}) async-start(), calls=%async_computation.7 | async-start | bytes 16842752 | tf_op jit(solution)/shard_map/all_gather | solution.py:167
  72.9 75.4 %all-to-all-start.3 = ((f32[16,64,1024]{2,1,0:T(8,128)}), f32[16,64,1024]{2,1,0:T(8,128)}, u32[]{:S(2)}, u32[]{:S(2)}) async-start(f32[16,64,1024]{2,1,0:T(8,128)} %broadcast_in_dim.10), calls=%async_computation.3 | async-start | bytes 8388608 | tf_op jit(solution)/shard_map/all_to_all | solution.py:159
  83.1 123.9 %copy-start.4 = (f32[1024,64]{0,1:T(8,128)S(1)}, f32[1024,64]{0,1:T(8,128)}, u32[]{:S(2)}) copy-start(f32[1024,64]{0,1:T(8,128)} %param.6) | copy-start | bytes 786436
  148.3 58.7 %all-to-all-start.4 = ((bf16[1,512,16,128]{3,1,0,2:T(8,128)(2,1)}), bf16[1,512,16,128]{3,1,0,2:T(8,128)(2,1)S(1)}, u32[]{:S(2)}, u32[]{:S(2)}) async-start(bf16[1,512,16,128]{3,1,0,2:T(8,128)(2,1)} %copy.11), calls=%async_computation.4 | async-start | bytes 4194304 | tf_op jit(solution)/shard_map/all_to_all | solution.py:175
  207.0 2.6 copy-start.2
  209.6 5.1 %copy-start.1 = (s32[8]{0:T(128)S(1)}, s32[8]{0:T(128)}, u32[]{:S(2)}) copy-start(s32[8]{0:T(128)} %order_ref.1) | copy-start | bytes 100
  209.6 101.2 %all-to-all-start.6 = ((f32[16,64,1024]{2,1,0:T(8,128)}), f32[16,64,1024]{2,1,0:T(8,128)}, u32[]{:S(2)}, u32[]{:S(2)}) async-start(f32[16,64,1024]{2,1,0:T(8,128)} %broadcast_in_dim.11), calls=%async_computation.6 | async-start | bytes 8388608 | tf_op jit(solution)/shard_map/all_to_all | solution.py:159
  287.2 2.0 copy-start
  310.9 25.9 %all-to-all-start.5 = ((f32[16,64,128]{2,1,0:T(8,128)}), f32[16,64,128]{2,1,0:T(8,128)S(1)}, u32[]{:S(2)}, u32[]{:S(2)}) async-start(f32[16,64,128]{2,1,0:T(8,128)} %bitcast.20), calls=%async_computation.5 | async-start | bytes 1048576 | tf_op jit(solution)/shard_map/all_to_all | solution.py:184
Sparse Core Ops, SparseCore 0:
  11.6 165.9 all-gather.2

commit v2 on v1

v2 whole, which is shorter than its diff:
```python
import functools

import jax
import jax.numpy as jnp
from jax import lax
from jax.experimental import pallas as pl
from jax.experimental.pallas import tpu as pltpu
from jax.sharding import PartitionSpec as P

f32 = jnp.float32
NB = 128
HIGH = lax.Precision.HIGHEST

def lanes(x):
    return jnp.broadcast_to(x, (8, NB))

def factor_blocks(blocks):
    lane = lax.broadcasted_iota(jnp.int32, (8, NB), 1)
    sub = lax.broadcasted_iota(jnp.int32, (8, NB), 0)
    at = [sub == k for k in range(8)]
    outs = [[] for _ in blocks]
    for j in range(16):
        lo = 8 * j
        inside = (lane >= lo) & (lane < lo + 8)
        unit = jnp.where(lane - lo == sub, 1.0, 0.0).astype(f32)
        for b, rows in enumerate(blocks):
            R = rows[j]
            D = [lanes(R[:, lo + k:lo + k + 1]) for k in range(8)]
            E = {(a, m): lanes(D[m][a:a + 1, :]) for m in range(8) for a in range(m, 8)}
            R = jnp.where(inside, unit, R)
            t = [lanes(R[k:k + 1, :]) for k in range(8)]
            inv, low = [], {}
            out = jnp.zeros((8, NB), f32)
            for k in range(8):
                p = E[k, k]
                inv.append(pl.reciprocal(p, approx=False))
                out = jnp.where(at[k], t[k] * lax.rsqrt(p), out)
                for a in range(k + 1, 8):
                    low[a, k] = E[a, k] * inv[k]
                    t[a] = t[a] - low[a, k] * t[k]
                    for m in range(k + 1, a + 1):
                        E[a, m] = E[a, m] - low[a, k] * E[m, k]
            outs[b].append(jnp.where(lane <= lo + sub, out, 0.0))
            if j < 15:
                w = [t[k] * inv[k] for k in range(8)]
                for k in range(7, 0, -1):
                    for a in range(k):
                        w[a] = w[a] - low[k, a] * w[k]
                for i in range(j + 1, 16):
                    T = rows[i]
                    terms = [lanes(T[:, lo + k:lo + k + 1]) * w[k] for k in range(7, -1, -1)]
                    T = jnp.where(inside, 0.0, T)
                    for x in terms:
                        T = T - x
                    rows[i] = T
    return outs

def load_block(ref, k):
    o = pl.multiple_of(k * NB, NB)
    return [ref[pl.ds(pl.multiple_of(o + 8 * i, 8), 8), pl.ds(o, NB)] for i in range(16)]

def split3(x):
    a = x.astype(jnp.bfloat16)
    r = x - a.astype(f32)
    b = r.astype(jnp.bfloat16)
    return a, b, (r - b.astype(f32)).astype(jnp.bfloat16)

def stack_left(x):
    a, b, c = split3(x)
    return jnp.concatenate([a, a, b, b, a, c], 1)

def stack_right(x):
    a, b, c = split3(x)
    return jnp.concatenate([a, b, a, b, c, a], 0)

def prepare(ref, inv_ref, right, k, n):
    o = pl.multiple_of(k * NB, NB)
    eye = jnp.where(lax.broadcasted_iota(jnp.int32, (NB, NB), 0) == lax.broadcasted_iota(jnp.int32, (NB, NB), 1), 1.0, 0.0).astype(f32)
    ref[pl.ds(o, NB), pl.ds(o, NB)] = eye
    left = stack_left(inv_ref[...])
    for h in range(n // 4):
        s = slice(h * 512, h * 512 + 512)
        U = jnp.dot(left, stack_right(ref[pl.ds(o, NB), s]), preferred_element_type=f32)
        ref[pl.ds(o, NB), s] = U
        right[:, s] = stack_right(U)

def eliminate(ref, right, k, n):
    for c in range(n - 1):
        @pl.when(k == c)
        def _():
            o, d = c * NB, (c + 1) * NB
            left = stack_left(ref[o:d, d:n * NB].T)
            ref[d:n * NB, o:d] = jnp.zeros((n * NB - d, NB), f32)
            if (n - 1 - c) < 4:
                ref[d:n * NB, :] -= jnp.dot(left, right[:, :n * NB], preferred_element_type=f32)
            else:
                m = (c + 1 + n) // 2 * NB
                ref[d:m, :] -= jnp.dot(left[:m - d], right[:, :n * NB], preferred_element_type=f32)
                ref[m:n * NB, :d] -= jnp.dot(left[m - d:], right[:, :d], preferred_element_type=f32)
                ref[m:n * NB, m:] -= jnp.dot(left[m - d:], right[:, m:n * NB], preferred_element_type=f32)

def kernel(tokens, order_ref, own_ref, g_ref, x_ref, m_ref, at, inv1, inv2, hst, right):
    r = lax.broadcasted_iota(jnp.int32, (NB, NB), 0)
    c = lax.broadcasted_iota(jnp.int32, (NB, NB), 1)
    diag = r == c
    tot = jnp.zeros((NB, NB), f32)
    for b in range(8):
        tot += jnp.where(diag, g_ref[b * NB:(b + 1) * NB, :NB], 0.0)
    scale = 1.0 / tokens
    damp = jnp.sum(tot) * (0.01 / 1024.0 / tokens)
    for a in range(8):
        for b in range(a, 8):
            if b - a <= 4:
                v = g_ref[a * NB:(a + 1) * NB, (b - a) * NB:(b - a + 1) * NB]
            else:
                v = g_ref[b * NB:(b + 1) * NB, (8 + a - b) * NB:(9 + a - b) * NB].T
            v = v * scale
            if a == b:
                v = v + jnp.where(diag, damp, 0.0)
            x_ref[a * NB:(a + 1) * NB, b * NB:(b + 1) * NB] = v
    for a in range(4):
        ta, sa = order_ref[4 + a], order_ref[a]
        oa = pl.multiple_of(ta * NB, NB)
        os = pl.multiple_of(sa * NB, NB)
        for b in range(4):
            tb = order_ref[4 + b]
            ob = pl.multiple_of(tb * NB, NB)
            if a <= b:
                at[a * NB:(a + 1) * NB, b * NB:(b + 1) * NB] = x_ref[pl.ds(oa, NB), pl.ds(ob, NB)]

            @pl.when(sa < tb)
            def _():
                hst[a * NB:(a + 1) * NB, b * NB:(b + 1) * NB] = x_ref[pl.ds(os, NB), pl.ds(ob, NB)]

            @pl.when(sa > tb)
            def _():
                hst[a * NB:(a + 1) * NB, b * NB:(b + 1) * NB] = x_ref[pl.ds(ob, NB), pl.ds(os, NB)].T

    def both(k, _):
        o1, o2 = factor_blocks([load_block(x_ref, k), load_block(at, k)])
        for i in range(16):
            inv1[8 * i:8 * i + 8, :] = o1[i]
            inv2[8 * i:8 * i + 8, :] = o2[i]
        prepare(x_ref, inv1, right, k, 8)
        eliminate(x_ref, right, k, 8)
        prepare(at, inv2, right, k, 4)
        eliminate(at, right, k, 4)
        return 0
    lax.fori_loop(0, 4, both, 0)

    def single(k, _):
        o1, = factor_blocks([load_block(x_ref, k)])
        for i in range(16):
            inv1[8 * i:8 * i + 8, :] = o1[i]
        prepare(x_ref, inv1, right, k, 8)
        eliminate(x_ref, right, k, 8)
        return 0
    lax.fori_loop(4, 8, single, 0)
    for k in range(7):
        x_ref[k * NB:(k + 1) * NB, (k + 1) * NB:] = jnp.zeros((NB, (7 - k) * NB), f32)
    for k in range(3):
        at[k * NB:(k + 1) * NB, (k + 1) * NB:] = jnp.zeros((NB, (3 - k) * NB), f32)
    own = own_ref[0]
    for a in range(4):
        @pl.when(order_ref[a] == own)
        def _():
            m_ref[...] = jnp.zeros((512, NB), f32)
            m_ref[a * NB:(a + 1) * NB, :] = jnp.where(diag, 1.0, 0.0)
        @pl.when(order_ref[4 + a] == own)
        def _():
            z = lax.dot_general(at[...], at[:, a * NB:(a + 1) * NB], (((0,), (0,)), ((), ())), precision=HIGH, preferred_element_type=f32)
            m_ref[...] = -jnp.dot(hst[...], z, precision=HIGH, preferred_element_type=f32)

def factor_call(gram, order, own, tokens):
    return pl.pallas_call(
        functools.partial(kernel, tokens),
        out_shape=(jax.ShapeDtypeStruct((1024, 1024), f32), jax.ShapeDtypeStruct((512, NB), f32)),
        in_specs=[pl.BlockSpec(memory_space=pltpu.SMEM), pl.BlockSpec(memory_space=pltpu.SMEM), pl.BlockSpec(memory_space=pltpu.VMEM)],
        out_specs=(pl.BlockSpec(memory_space=pltpu.VMEM), pl.BlockSpec(memory_space=pltpu.VMEM)),
        scratch_shapes=[pltpu.VMEM((512, 512), f32), pltpu.VMEM((NB, NB), f32), pltpu.VMEM((NB, NB), f32), pltpu.VMEM((512, 512), f32), pltpu.VMEM((768, 1024), jnp.bfloat16)],
        compiler_params=pltpu.CompilerParams(vmem_limit_bytes=40 * 1024 * 1024),
    )(order, own, gram)


def slab_kernel(tokens, panel_ref, trail_ref, inverse_ref, out_ref, total):
    @pl.when(pl.program_id(0) == 0)
    def _():
        total[...] = jnp.zeros_like(total)

    for g in range(panel_ref.shape[0]):
        total[...] += jnp.dot(panel_ref[g], trail_ref[g], preferred_element_type=f32)

    @pl.when(pl.program_id(0) == pl.num_programs(0) - 1)
    def _():
        slab = total[...] * (1.0 / tokens)
        for h in range(4):
            s = slice(256 * h, 256 * h + 256)
            e = 256 * h + 256
            out_ref[s, :] = jnp.dot(inverse_ref[s, :e], slab[:e], precision=HIGH, preferred_element_type=f32)


def slab_call(panel, trail, inverse, tokens):
    groups, channels, span = panel.shape
    columns = trail.shape[2]
    each = 2
    return pl.pallas_call(
        functools.partial(slab_kernel, tokens),
        grid=(groups // each,),
        in_specs=[
            pl.BlockSpec((each, channels, span), lambda i: (i, 0, 0)),
            pl.BlockSpec((each, span, columns), lambda i: (i, 0, 0)),
            pl.BlockSpec((channels, channels), lambda i: (0, 0)),
        ],
        out_specs=pl.BlockSpec((channels, columns), lambda i: (0, 0)),
        out_shape=jax.ShapeDtypeStruct((channels, columns), f32),
        scratch_shapes=[pltpu.VMEM((channels, columns), f32)],
        compiler_params=pltpu.CompilerParams(vmem_limit_bytes=40 * 1024 * 1024),
    )(panel, trail, inverse)


def spread(x, axis):
    n = lax.axis_size(axis)
    return lax.all_to_all(jnp.broadcast_to(x[None], (n,) + x.shape), axis, 0, 0)


def ascending(blocks):
    place = jnp.sum((blocks[None, :] < blocks[:, None]).astype(jnp.int32), 1)
    slot = jnp.arange(blocks.shape[0], dtype=jnp.int32)
    return jnp.sum(jnp.where(place[None, :] == slot[:, None], blocks[None, :], 0), 1)


def on_device(acts_panel, acts_trail, weight_panel, block_order):
    n_row = lax.axis_size("row")
    span, own_n = acts_panel.shape
    tokens = span * n_row
    own = lax.axis_index("col")
    own_t = acts_panel.T
    everything = lax.all_gather(own_t, ("row", "col"))
    panel_t = spread(own_t, "col").reshape(-1, span)
    strip = lax.dot_general(own_t, panel_t, (((1,), (1,)), ((), ())), preferred_element_type=f32)
    pieces = strip.reshape(8, 8, 2, 512).transpose(0, 2, 1, 3).reshape(16, 8, 512)
    piece = lax.all_to_all(pieces, "row", 0, 0).sum(0)
    strip_total = spread(piece, "row").reshape(8, 2, 8, 512).transpose(0, 2, 1, 3).reshape(64, 1024)
    twice = jnp.concatenate([strip_total, strip_total[:, :512]], 1)
    band = lax.dynamic_slice_in_dim(twice, own // 2 * NB, 5 * NB, 1)
    gram = spread(band, "col").reshape(1024, 5 * NB)
    weight_t = weight_panel.T
    columns = acts_trail.shape[1] // n_row
    trail_cut = acts_trail.reshape(span, n_row, columns).transpose(1, 0, 2)
    weight_in, trail_cut, gram = lax.optimization_barrier((weight_t, trail_cut, gram))
    trail = lax.all_to_all(trail_cut, "row", 0, 0)
    weight_all = lax.all_gather(weight_in, "col", axis=0, tiled=True)
    order = jnp.concatenate([block_order[:4], ascending(block_order[4:])])
    inverse_factor, mixing = factor_call(gram, order, (own // 2).reshape(1), tokens)
    everything, trail, mixing = lax.optimization_barrier((everything, trail, mixing))
    solved = slab_call(everything.reshape(n_row, 1024, span), trail, inverse_factor, tokens)
    solved, weight_all = lax.optimization_barrier((solved, weight_all))
    slab_rows = lax.all_to_all(solved.reshape(n_row, 1024 // n_row, -1), "row", 0, 0)
    slab_factor = slab_rows.transpose(1, 0, 2).reshape(1024 // n_row, -1)
    pruned = jnp.concatenate(
        [lax.dynamic_slice_in_dim(weight_all, block_order[q] * NB, NB, 0) for q in range(4)], 0
    )
    own_mixing = lax.dynamic_slice_in_dim(mixing, (own % 2) * own_n, own_n, 1)
    change = lax.dot_general(own_mixing, pruned, (((0,), (0,)), ((), ())), precision=HIGH)
    return (slab_factor, (weight_t - change).T)


def solution(mesh):
    return jax.shard_map(
        on_device,
        mesh=mesh,
        in_specs=(P("row", "col"), P("row", "col"), P("row", "col"), P()),
        out_specs=(P("row", "col"), P("row", "col")),
        check_vma=False,
    )
```

time: 349 us -> 268 us (0.77)
  waiting for transfers between devices: 133 us -> 82.9 us
  blocking collectives: 61 us -> 44.4 us
  Pallas kernels: 87.6 us -> 75.6 us
  matrix products: 9.18 us -> 2.67 us
    all_to_all x1, waiting for transfers between devices: 55 us -> 0.01 us  [on_device(): trail = lax.all_to_all(trail_cut, 'row', 0, 0)]
    all_gather x0 -> x1, waiting for transfers between devices: none -> 20.1 us  [on_device(): weight_all = lax.all_gather(weight_in, 'col', axis=0, tiled=True)]
    all_to_all x2 -> x1, blocking collectives: 35.6 us -> 19 us  [spread(): return lax.all_to_all(jnp.broadcast_to(x[None], (n,) + x.shape), axis, 0, 0)]
    all_to_all x2, waiting for transfers between devices: 65.2 us -> 49.6 us  [spread(): return lax.all_to_all(jnp.broadcast_to(x[None], (n,) + x.shape), axis, 0, 0)]
    pallas_call x1, Pallas kernels: 72.4 us -> 61.9 us  [factor_call(): pl.pallas_call(functools.partial(kernel, tokens), out_shape=(jax.ShapeDty...]
    dot_general x1 -> x0, matrix products: 6.51 us -> none  [on_device(): solved = jnp.dot(inverse_factor, slab, precision=HIGH)]
    unnamed x10 -> x11, local copies, waits for them, and re-layouts: 1.98 us -> 8.13 us
    reshape x0 -> x1, local copies, waits for them, and re-layouts: none -> 3.91 us  [on_device(): trail_cut = acts_trail.reshape(span, n_row, columns).transpose(1, 0, 2)]
  transfers between devices with their start and end apart: 5 -> 6, of which waited for: 3 -> 4; matrix products, arithmetic and copies ran while one was open for 7% -> 6% of each run, Pallas kernels for 25% -> 29%
where the time goes in v2:
time: 268 us; the launch traced here: 264 us
  waiting for transfers between devices  82.9 us (31%)
  Pallas kernels  75.6 us (28%)
  blocking collectives  44.4 us (17%)
  starting transfers between devices  21.7 us (8%)
  local copies, waits for them, and re-layouts  18.7 us (7%)
  between operations  17.1 us (6%)
    pallas_call x1, Pallas kernels, factor_call(): pl.pallas_call(functools.partial(kernel, tokens), out_shape=(jax.ShapeDty...  61.9 us
    all_to_all x2, waiting for transfers between devices, spread(): return lax.all_to_all(jnp.broadcast_to(x[None], (n,) + x.shape), axis, 0, 0)  49.6 us
    all_to_all x1, blocking collectives, on_device(): piece = lax.all_to_all(pieces, 'row', 0, 0).sum(0)  25.5 us
    all_gather x1, waiting for transfers between devices, on_device(): weight_all = lax.all_gather(weight_in, 'col', axis=0, tiled=True)  20.1 us
    all_to_all x1, blocking collectives, spread(): return lax.all_to_all(jnp.broadcast_to(x[None], (n,) + x.shape), axis, 0, 0)  19 us
    pallas_call x1, Pallas kernels, slab_call(): pl.pallas_call(functools.partial(slab_kernel, tokens), grid=(groups // ea...  13.6 us
    all_to_all x1, waiting for transfers between devices, on_device(): lax.all_to_all(solved.reshape(n_row, 1024 // n_row, -1), 'row', 0, 0)  12.5 us
    all_to_all x1, starting transfers between devices, on_device(): lax.all_to_all(solved.reshape(n_row, 1024 // n_row, -1), 'row', 0, 0)  9.13 us
  transfers between devices with their start and end apart: 6, of which 4 were waited for; matrix products, arithmetic and copies ran while one was open for 6% of the time, Pallas kernels for 29%

profile of v2, /device:TPU:2, one launch (start us, length us, event | category | flops | bytes accessed | tf_op | source)
XLA Modules:
  0.0 263.6 jit_solution(736272302473691038)
XLA Ops:
  7.2 0.0 copy-start.2
  7.2 0.0 all-gather.6.cloned.1.call-start
  7.2 0.7 all-gather.6.cloned.1.call-update
  7.9 0.9 broadcast_in_dim.12
  8.8 19.0 %all_to_all.30 = bf16[16,64,512]{2,1,0:T(8,128)(2,1)S(1)} all-to-all(bf16[16,64,512]{2,1,0:T(8,128)(2,1)S(1)} %broadcast_in_dim.12), channel_id=1, replica_groups=mesh['row'=16,'col'=16] {'col'}, dimensions={0} | all-to-all | bytes 2097152 | tf_op jit(solution)/shard_map/all_to_all | solution.py:223
  27.8 0.0 copy-done.2
  27.8 0.4 fusion.13
  28.3 25.5 %all_to_all.31 = f32[16,8,512]{2,1,0:T(8,128)S(1)} all-to-all(f32[16,8,512]{2,1,0:T(8,128)S(1)} %bitcast.46), channel_id=1, replica_groups=mesh['row'=16,'col'=16] {'row'}, dimensions={0} | all-to-all | bytes 524288 | tf_op jit(solution)/shard_map/all_to_all | solution.py:242
  53.8 0.7 broadcast_in_dim.13
  54.5 3.5 %all-to-all-start.2 = ((f32[16,8,512]{2,1,0:T(8,128)}), f32[16,8,512]{2,1,0:T(8,128)S(1)}, u32[]{:S(2)}, u32[]{:S(2)}) async-start(f32[16,8,512]{2,1,0:T(8,128)} %broadcast_in_dim.13), calls=%async_computation.2 | async-start | bytes 524288 | tf_op jit(solution)/shard_map/all_to_all | solution.py:223
  58.0 14.2 %all-to-all-done.2 = f32[16,8,512]{2,1,0:T(8,128)S(1)} async-done(((f32[16,8,512]{2,1,0:T(8,128)}), f32[16,8,512]{2,1,0:T(8,128)S(1)}, u32[]{:S(2)}, u32[]{:S(2)}) %all-to-all-start.2) | async-done | bytes 262176 | tf_op jit(solution)/shard_map/all_to_all | solution.py:223
  72.3 1.8 broadcast_in_dim.14
  74.1 4.5 %all-to-all-start.3 = ((f32[16,64,640]{2,1,0:T(8,128)}), f32[16,64,640]{2,1,0:T(8,128)S(1)}, u32[]{:S(2)}, u32[]{:S(2)}) async-start(f32[16,64,640]{2,1,0:T(8,128)} %broadcast_in_dim.14), calls=%async_computation.3 | async-start | bytes 5242880 | tf_op jit(solution)/shard_map/all_to_all | solution.py:223
  78.6 0.0 all-gather.4.cloned.1.call-start
  78.6 4.0 %copy.10 = bf16[512,2048]{0,1:T(8,128)(2,1)} copy(bf16[512,2048]{1,0:T(8,128)(2,1)} %param.5) | data formatting | bytes 4194304 | tf_op args[1]
  82.6 3.9 %copy.11 = bf16[512,16,128]{2,0,1:T(8,128)(2,1)} copy(bf16[512,16,128]{0,2,1:T(8,128)(2,1)} %bitcast.42) | data formatting | bytes 4194304 | tf_op jit(solution)/shard_map/reshape | solution.py:249
  86.5 35.4 %all-to-all-done.3 = f32[16,64,640]{2,1,0:T(8,128)S(1)} async-done(((f32[16,64,640]{2,1,0:T(8,128)}), f32[16,64,640]{2,1,0:T(8,128)S(1)}, u32[]{:S(2)}, u32[]{:S(2)}) %all-to-all-start.3) | async-done | bytes 2621472 | tf_op jit(solution)/shard_map/all_to_all | solution.py:223
  121.9 0.0 all-gather.4.cloned.1.call-update
  122.0 0.0 copy-start.4
  122.0 4.5 %all-to-all-start.4 = ((bf16[16,512,128]{2,1,0:T(8,128)(2,1)}), bf16[16,512,128]{2,1,0:T(8,128)(2,1)}, u32[]{:S(2)}, u32[]{:S(2)}) async-start(bf16[16,512,128]{2,1,0:T(8,128)(2,1)} %bitcast.41), calls=%async_computation.4 | async-start | bytes 4194304 | tf_op jit(solution)/shard_map/all_to_all | solution.py:251
  126.4 0.0 copy-done.4
  126.5 0.1 fusion.18
  126.5 0.2 convert_reduce_fusion
  126.7 0.1 select_reduce_fusion
  126.8 0.1 pad_add_fusion.order_ref
  126.9 61.9 %shard_map.59 = (f32[1024,1024]{1,0:T(8,128)S(1)}, f32[512,128]{1,0:T(8,128)S(1)}) custom-call(s32[8]{0:T(128)S(1)} %pad_add_fusion.order_ref, s32[1]{0:T(128)} %bitcast.18.own_ref, f32[1024,640]{1,0:T(8,128)S(1)} %bitcast.39), custom_call_target="tpu_custom_call" | custom-call | tf_op jit(solution)/shard_map/pallas_call | solution.py:175
  188.9 0.0 copy-start
  188.9 2.0 copy-done
  190.8 0.0 all-to-all-done.4.trail_ref
  190.8 0.0 all-gather.6.cloned.1.call-done
  190.8 0.0 copy-start.1
  190.8 2.2 copy-done.1
  193.0 13.6 %shard_map.60 = f32[1024,128]{1,0:T(8,128)} custom-call(bf16[16,1024,512]{2,1,0:T(8,128)(2,1)} %bitcast.40, bf16[16,512,128]{2,1,0:T(8,128)(2,1)} %all-to-all-done.4.trail_ref, f32[1024,1024]{1,0:T(8,128)S(1)} %copy-done.1), custom_call_target="tpu_custom_call" | custom-call | tf_op jit(solution)/shard_map/pallas_call | solution.py:206
  206.6 20.1 %all-gather.4.cloned.1.call-done = f32[1024,1024]{1,0:T(8,128)} async-done(((f32[64,1024]{1,0:T(8,128)}), f32[1024,1024]{1,0:T(8,128)}) %all-gather.4.cloned.1.call-update) | async-done | bytes 4194320 | tf_op jit(solution)/shard_map/all_gather | solution.py:252
  226.8 9.1 %all-to-all-start.5 = ((f32[16,64,128]{2,1,0:T(8,128)}), f32[16,64,128]{2,1,0:T(8,128)S(1)}, u32[]{:S(2)}, u32[]{:S(2)}) async-start(f32[16,64,128]{2,1,0:T(8,128)} %bitcast.20), calls=%async_computation.5 | async-start | bytes 1048576 | tf_op jit(solution)/shard_map/all_to_all | solution.py:258
  235.9 0.6 fusion.17
  239.0 0.0 copy-start.3
  239.0 1.7 constant_dynamic-slice_fusion.3
  240.7 0.0 copy-done.3
  240.7 2.2 fusion.8
  243.0 12.5 %all-to-all-done.5 = f32[16,64,128]{2,1,0:T(8,128)S(1)} async-done(((f32[16,64,128]{2,1,0:T(8,128)}), f32[16,64,128]{2,1,0:T(8,128)S(1)}, u32[]{:S(2)}, u32[]{:S(2)}) %all-to-all-start.5) | async-done | bytes 524320 | tf_op jit(solution)/shard_map/all_to_all | solution.py:258
  255.5 0.8 copy_bitcast_fusion
  (3 shorter events, 0.1 us)
Async XLA Ops:
  7.2 20.7 %copy-start.2 = (bf16[512,64]{0,1:T(8,128)(2,1)S(1)}, bf16[512,64]{0,1:T(8,128)(2,1)}, u32[]{:S(2)}) copy-start(bf16[512,64]{0,1:T(8,128)(2,1)} %param.4) | copy-start | bytes 196612
  7.2 183.7 %all-gather.6.cloned.1.call-start = ((), (), s32[]{:S(2)}) async-start(), calls=%async_computation.7 | async-start | bytes 16842752 | tf_op jit(solution)/shard_map/all_gather | solution.py:238
  54.5 17.8 %all-to-all-start.2 = ((f32[16,8,512]{2,1,0:T(8,128)}), f32[16,8,512]{2,1,0:T(8,128)S(1)}, u32[]{:S(2)}, u32[]{:S(2)}) async-start(f32[16,8,512]{2,1,0:T(8,128)} %broadcast_in_dim.13), calls=%async_computation.2 | async-start | bytes 524288 | tf_op jit(solution)/shard_map/all_to_all | solution.py:223
  74.1 47.8 %all-to-all-start.3 = ((f32[16,64,640]{2,1,0:T(8,128)}), f32[16,64,640]{2,1,0:T(8,128)S(1)}, u32[]{:S(2)}, u32[]{:S(2)}) async-start(f32[16,64,640]{2,1,0:T(8,128)} %broadcast_in_dim.14), calls=%async_computation.3 | async-start | bytes 5242880 | tf_op jit(solution)/shard_map/all_to_all | solution.py:223
  78.6 148.2 %all-gather.4.cloned.1.call-start = ((), (), s32[]{:S(2)}) async-start(), calls=%async_computation.6 | async-start | bytes 4456448 | tf_op jit(solution)/shard_map/all_gather | solution.py:252
  122.0 4.5 %copy-start.4 = (s32[8]{0:T(128)S(1)}, s32[8]{0:T(128)}, u32[]{:S(2)}) copy-start(s32[8]{0:T(128)} %param.7) | copy-start | bytes 100
  122.0 68.9 %all-to-all-start.4 = ((bf16[16,512,128]{2,1,0:T(8,128)(2,1)}), bf16[16,512,128]{2,1,0:T(8,128)(2,1)}, u32[]{:S(2)}, u32[]{:S(2)}) async-start(bf16[16,512,128]{2,1,0:T(8,128)(2,1)} %bitcast.41), calls=%async_computation.4 | async-start | bytes 4194304 | tf_op jit(solution)/shard_map/all_to_all | solution.py:251
  188.9 2.0 copy-start
  190.8 2.2 copy-start.1
  226.8 28.7 %all-to-all-start.5 = ((f32[16,64,128]{2,1,0:T(8,128)}), f32[16,64,128]{2,1,0:T(8,128)S(1)}, u32[]{:S(2)}, u32[]{:S(2)}) async-start(f32[16,64,128]{2,1,0:T(8,128)} %bitcast.20), calls=%async_computation.5 | async-start | bytes 1048576 | tf_op jit(solution)/shard_map/all_to_all | solution.py:258
  239.0 1.7 copy-start.3
Sparse Core Ops, SparseCore 0:
  11.6 174.0 all-gather.5
  187.6 39.1 all-gather.3

commit v3 on v2

--- a/solution.py
+++ b/solution.py
@@ -73,33 +73,30 @@
     a, b, c = split3(x)
     return jnp.concatenate([a, b, a, b, c, a], 0)
 
-def prepare(ref, inv_ref, right, k, n):
+def prepare(ref, inv_ref, left, right, k, n):
     o = pl.multiple_of(k * NB, NB)
+    w = n * NB
     eye = jnp.where(lax.broadcasted_iota(jnp.int32, (NB, NB), 0) == lax.broadcasted_iota(jnp.int32, (NB, NB), 1), 1.0, 0.0).astype(f32)
     ref[pl.ds(o, NB), pl.ds(o, NB)] = eye
-    left = stack_left(inv_ref[...])
+    inverse = stack_left(inv_ref[...])
     for h in range(n // 4):
         s = slice(h * 512, h * 512 + 512)
-        U = jnp.dot(left, stack_right(ref[pl.ds(o, NB), s]), preferred_element_type=f32)
+        U = jnp.dot(inverse, stack_right(ref[pl.ds(o, NB), s]), preferred_element_type=f32)
         ref[pl.ds(o, NB), s] = U
         right[:, s] = stack_right(U)
-
-def eliminate(ref, right, k, n):
-    for c in range(n - 1):
-        @pl.when(k == c)
-        def _():
-            o, d = c * NB, (c + 1) * NB
-            left = stack_left(ref[o:d, d:n * NB].T)
-            ref[d:n * NB, o:d] = jnp.zeros((n * NB - d, NB), f32)
-            if (n - 1 - c) < 4:
-                ref[d:n * NB, :] -= jnp.dot(left, right[:, :n * NB], preferred_element_type=f32)
-            else:
-                m = (c + 1 + n) // 2 * NB
-                ref[d:m, :] -= jnp.dot(left[:m - d], right[:, :n * NB], preferred_element_type=f32)
-                ref[m:n * NB, :d] -= jnp.dot(left[m - d:], right[:, :d], preferred_element_type=f32)
-                ref[m:n * NB, m:] -= jnp.dot(left[m - d:], right[:, m:n * NB], preferred_element_type=f32)
-
-def kernel(tokens, order_ref, own_ref, g_ref, x_ref, m_ref, at, inv1, inv2, hst, right):
+    for i in range(1, n):
+        s = slice(i * NB, i * NB + NB)
+        below = k < i
+        left[s, :] = stack_left(jnp.where(below, ref[pl.ds(o, NB), s].T, 0.0))
+        ref[s, pl.ds(o, NB)] = jnp.where(below, 0.0, ref[s, pl.ds(o, NB)])
+    v = pl.multiple_of(jnp.minimum(k + 1, n - 1) * NB, NB)
+    ref[pl.ds(v, NB), pl.ds(v, NB)] -= jnp.dot(left[pl.ds(v, NB), :], right[:, pl.ds(v, NB)], preferred_element_type=f32)
+
+def update(ref, left, right, first, n):
+    s = slice(first * NB, n * NB)
+    ref[s, :] -= jnp.dot(left[s, :], right[...], preferred_element_type=f32)
+
+def kernel(tokens, order_ref, own_ref, g_ref, x_out, m_ref, x_ref, at, inv1, inv2, hst, left1, right1, left2, right2, sems):
     r = lax.broadcasted_iota(jnp.int32, (NB, NB), 0)
     c = lax.broadcasted_iota(jnp.int32, (NB, NB), 1)
     diag = r == c
@@ -136,28 +133,47 @@
             def _():
                 hst[a * NB:(a + 1) * NB, b * NB:(b + 1) * NB] = x_ref[pl.ds(ob, NB), pl.ds(os, NB)].T
 
+    left1[...] = jnp.zeros_like(left1)
+    right1[...] = jnp.zeros_like(right1)
+    left2[...] = jnp.zeros_like(left2)
+    right2[...] = jnp.zeros_like(right2)
+
+    def send(k):
+        o = pl.multiple_of(k * NB, NB)
+        return pltpu.make_async_copy(x_ref.at[pl.ds(o, NB), :], x_out.at[pl.ds(o, NB), :], sems.at[k])
+
+    def finish(k):
+        o = pl.multiple_of(k * NB, NB)
+
+        @pl.when(lax.rem(k, 2) == 0)
+        def _():
+            x_ref[pl.ds(o, NB), pl.ds(pl.multiple_of(o + NB, NB), NB)] = jnp.zeros((NB, NB), f32)
+        send(k).start()
+
     def both(k, _):
-        o1, o2 = factor_blocks([load_block(x_ref, k), load_block(at, k)])
+        b1, b2 = load_block(x_ref, k), load_block(at, k)
+        update(x_ref, left1, right1, 1, 8)
+        update(at, left2, right2, 1, 4)
+        o1, o2 = factor_blocks([b1, b2])
         for i in range(16):
             inv1[8 * i:8 * i + 8, :] = o1[i]
             inv2[8 * i:8 * i + 8, :] = o2[i]
-        prepare(x_ref, inv1, right, k, 8)
-        eliminate(x_ref, right, k, 8)
-        prepare(at, inv2, right, k, 4)
-        eliminate(at, right, k, 4)
+        prepare(x_ref, inv1, left1, right1, k, 8)
+        prepare(at, inv2, left2, right2, k, 4)
+        finish(k)
         return 0
     lax.fori_loop(0, 4, both, 0)
 
     def single(k, _):
-        o1, = factor_blocks([load_block(x_ref, k)])
+        b1 = load_block(x_ref, k)
+        update(x_ref, left1, right1, 4, 8)
+        o1, = factor_blocks([b1])
         for i in range(16):
             inv1[8 * i:8 * i + 8, :] = o1[i]
-        prepare(x_ref, inv1, right, k, 8)
-        eliminate(x_ref, right, k, 8)
+        prepare(x_ref, inv1, left1, right1, k, 8)
+        finish(k)
         return 0
     lax.fori_loop(4, 8, single, 0)
-    for k in range(7):
-        x_ref[k * NB:(k + 1) * NB, (k + 1) * NB:] = jnp.zeros((NB, (7 - k) * NB), f32)
     for k in range(3):
         at[k * NB:(k + 1) * NB, (k + 1) * NB:] = jnp.zeros((NB, (3 - k) * NB), f32)
     own = own_ref[0]
@@ -170,33 +186,46 @@
         def _():
             z = lax.dot_general(at[...], at[:, a * NB:(a + 1) * NB], (((0,), (0,)), ((), ())), precision=HIGH, preferred_element_type=f32)
             m_ref[...] = -jnp.dot(hst[...], z, precision=HIGH, preferred_element_type=f32)
+    for k in range(8):
+        send(k).wait()
 
 def factor_call(gram, order, own, tokens):
+    bf16 = jnp.bfloat16
     return pl.pallas_call(
         functools.partial(kernel, tokens),
         out_shape=(jax.ShapeDtypeStruct((1024, 1024), f32), jax.ShapeDtypeStruct((512, NB), f32)),
         in_specs=[pl.BlockSpec(memory_space=pltpu.SMEM), pl.BlockSpec(memory_space=pltpu.SMEM), pl.BlockSpec(memory_space=pltpu.VMEM)],
-        out_specs=(pl.BlockSpec(memory_space=pltpu.VMEM), pl.BlockSpec(memory_space=pltpu.VMEM)),
-        scratch_shapes=[pltpu.VMEM((512, 512), f32), pltpu.VMEM((NB, NB), f32), pltpu.VMEM((NB, NB), f32), pltpu.VMEM((512, 512), f32), pltpu.VMEM((768, 1024), jnp.bfloat16)],
+        out_specs=(pl.BlockSpec(memory_space=pltpu.MemorySpace.HBM), pl.BlockSpec(memory_space=pltpu.VMEM)),
+        scratch_shapes=[
+            pltpu.VMEM((1024, 1024), f32), pltpu.VMEM((512, 512), f32), pltpu.VMEM((NB, NB), f32), pltpu.VMEM((NB, NB), f32),
+            pltpu.VMEM((512, 512), f32), pltpu.VMEM((1024, 768), bf16), pltpu.VMEM((768, 1024), bf16),
+            pltpu.VMEM((512, 768), bf16), pltpu.VMEM((768, 512), bf16), pltpu.SemaphoreType.DMA((8,)),
+        ],
         compiler_params=pltpu.CompilerParams(vmem_limit_bytes=40 * 1024 * 1024),
     )(order, own, gram)
 
 
-def slab_kernel(tokens, panel_ref, trail_ref, inverse_ref, out_ref, total):
+def slab_kernel(tokens, panel_ref, trail_ref, inverse_ref, out_ref, total, inverse, sem):
+    copy = pltpu.make_async_copy(inverse_ref, inverse, sem)
+
     @pl.when(pl.program_id(0) == 0)
     def _():
+        copy.start()
         total[...] = jnp.zeros_like(total)
 
-    for g in range(panel_ref.shape[0]):
-        total[...] += jnp.dot(panel_ref[g], trail_ref[g], preferred_element_type=f32)
+    part = jnp.dot(panel_ref[0], trail_ref[0], preferred_element_type=f32)
+    for g in range(1, panel_ref.shape[0]):
+        part += jnp.dot(panel_ref[g], trail_ref[g], preferred_element_type=f32)
+    total[...] += part
 
     @pl.when(pl.program_id(0) == pl.num_programs(0) - 1)
     def _():
+        copy.wait()
         slab = total[...] * (1.0 / tokens)
         for h in range(4):
             s = slice(256 * h, 256 * h + 256)
             e = 256 * h + 256
-            out_ref[s, :] = jnp.dot(inverse_ref[s, :e], slab[:e], precision=HIGH, preferred_element_type=f32)
+            out_ref[s, :] = jnp.dot(inverse[s, :e], slab[:e], precision=HIGH, preferred_element_type=f32)
 
 
 def slab_call(panel, trail, inverse, tokens):
@@ -209,11 +238,15 @@
         in_specs=[
             pl.BlockSpec((each, channels, span), lambda i: (i, 0, 0)),
             pl.BlockSpec((each, span, columns), lambda i: (i, 0, 0)),
-            pl.BlockSpec((channels, channels), lambda i: (0, 0)),
+            pl.BlockSpec(memory_space=pltpu.MemorySpace.HBM),
         ],
         out_specs=pl.BlockSpec((channels, columns), lambda i: (0, 0)),
         out_shape=jax.ShapeDtypeStruct((channels, columns), f32),
-        scratch_shapes=[pltpu.VMEM((channels, columns), f32)],
+        scratch_shapes=[
+            pltpu.VMEM((channels, columns), f32),
+            pltpu.VMEM((channels, channels), f32),
+            pltpu.SemaphoreType.DMA,
+        ],
         compiler_params=pltpu.CompilerParams(vmem_limit_bytes=40 * 1024 * 1024),
     )(panel, trail, inverse)
 
@@ -254,7 +287,6 @@
     inverse_factor, mixing = factor_call(gram, order, (own // 2).reshape(1), tokens)
     everything, trail, mixing = lax.optimization_barrier((everything, trail, mixing))
     solved = slab_call(everything.reshape(n_row, 1024, span), trail, inverse_factor, tokens)
-    solved, weight_all = lax.optimization_barrier((solved, weight_all))
     slab_rows = lax.all_to_all(solved.reshape(n_row, 1024 // n_row, -1), "row", 0, 0)
     slab_factor = slab_rows.transpose(1, 0, 2).reshape(1024 // n_row, -1)
     pruned = jnp.concatenate(

time: 268 us -> 244 us (0.910); the launches traced: 264 us -> 244 us
  waiting for transfers between devices: 82.9 us -> 62.3 us
    all_gather x1, waiting for transfers between devices: 20.1 us -> 8.41 us  [on_device(): weight_all = lax.all_gather(weight_in, 'col', axis=0, tiled=True)]
    all_to_all x1, waiting for transfers between devices: 12.5 us -> 3.51 us  [on_device(): lax.all_to_all(solved.reshape(n_row, 1024 // n_row, -1), 'row', 0, 0)]
  transfers between devices with their start and end apart: 6 -> 6, of which waited for: 4 -> 4; matrix products, arithmetic and copies ran while one was open for 6% -> 7% of each run, Pallas kernels for 29% -> 31%
where the time goes in v3:
time: 244 us
  Pallas kernels  76.3 us (31%)
  waiting for transfers between devices  62.3 us (26%)
  blocking collectives  44.4 us (18%)
  starting transfers between devices  22.1 us (9%)
  local copies, waits for them, and re-layouts  18.6 us (8%)
  between operations  16.7 us (7%)
  matrix products  2.67 us (1%)
    pallas_call x1, Pallas kernels, factor_call(): pl.pallas_call(functools.partial(kernel, tokens), out_shape=(jax.ShapeDty...  62.4 us
    all_to_all x2, waiting for transfers between devices, spread(): return lax.all_to_all(jnp.broadcast_to(x[None], (n,) + x.shape), axis, 0, 0)  49.6 us
    all_to_all x1, blocking collectives, on_device(): piece = lax.all_to_all(pieces, 'row', 0, 0).sum(0)  25.5 us
    all_to_all x1, blocking collectives, spread(): return lax.all_to_all(jnp.broadcast_to(x[None], (n,) + x.shape), axis, 0, 0)  19 us
    pallas_call x1, Pallas kernels, slab_call(): pl.pallas_call(functools.partial(slab_kernel, tokens), grid=(groups // ea...  13.9 us
    all_to_all x1, starting transfers between devices, on_device(): lax.all_to_all(solved.reshape(n_row, 1024 // n_row, -1), 'row', 0, 0)  9.5 us
    all_gather x1, waiting for transfers between devices, on_device(): weight_all = lax.all_gather(weight_in, 'col', axis=0, tiled=True)  8.41 us
    unnamed x11, local copies, waits for them, and re-layouts  8.13 us
  transfers between devices with their start and end apart: 6, of which 4 were waited for; matrix products, arithmetic and copies ran while one was open for 7% of the time, Pallas kernels for 31%

profile of v3, /device:TPU:2, one launch (start us, length us, event | category | flops | bytes accessed | tf_op | source)
XLA Modules:
  0.0 243.6 jit_solution(7603790933517066078)
XLA Ops:
  7.2 0.0 copy-start.2
  7.2 0.0 all-gather.6.cloned.1.call-start
  7.2 0.7 all-gather.6.cloned.1.call-update
  7.9 0.9 broadcast_in_dim.12
  8.8 19.0 %all_to_all.30 = bf16[16,64,512]{2,1,0:T(8,128)(2,1)S(1)} all-to-all(bf16[16,64,512]{2,1,0:T(8,128)(2,1)S(1)} %broadcast_in_dim.12), channel_id=1, replica_groups=mesh['row'=16,'col'=16] {'col'}, dimensions={0} | all-to-all | bytes 2097152 | tf_op jit(solution)/shard_map/all_to_all | solution.py:256
  27.8 0.0 copy-done.2
  27.8 0.4 fusion.13
  28.3 25.5 %all_to_all.31 = f32[16,8,512]{2,1,0:T(8,128)S(1)} all-to-all(f32[16,8,512]{2,1,0:T(8,128)S(1)} %bitcast.46), channel_id=1, replica_groups=mesh['row'=16,'col'=16] {'row'}, dimensions={0} | all-to-all | bytes 524288 | tf_op jit(solution)/shard_map/all_to_all | solution.py:275
  53.8 0.7 broadcast_in_dim.13
  54.5 3.5 %all-to-all-start.2 = ((f32[16,8,512]{2,1,0:T(8,128)}), f32[16,8,512]{2,1,0:T(8,128)S(1)}, u32[]{:S(2)}, u32[]{:S(2)}) async-start(f32[16,8,512]{2,1,0:T(8,128)} %broadcast_in_dim.13), calls=%async_computation.2 | async-start | bytes 524288 | tf_op jit(solution)/shard_map/all_to_all | solution.py:256
  58.0 14.2 %all-to-all-done.2 = f32[16,8,512]{2,1,0:T(8,128)S(1)} async-done(((f32[16,8,512]{2,1,0:T(8,128)}), f32[16,8,512]{2,1,0:T(8,128)S(1)}, u32[]{:S(2)}, u32[]{:S(2)}) %all-to-all-start.2) | async-done | bytes 262176 | tf_op jit(solution)/shard_map/all_to_all | solution.py:256
  72.3 1.8 broadcast_in_dim.14
  74.1 4.5 %all-to-all-start.3 = ((f32[16,64,640]{2,1,0:T(8,128)}), f32[16,64,640]{2,1,0:T(8,128)S(1)}, u32[]{:S(2)}, u32[]{:S(2)}) async-start(f32[16,64,640]{2,1,0:T(8,128)} %broadcast_in_dim.14), calls=%async_computation.3 | async-start | bytes 5242880 | tf_op jit(solution)/shard_map/all_to_all | solution.py:256
  78.6 0.0 all-gather.4.cloned.1.call-start
  78.6 4.0 %copy.10 = bf16[512,2048]{0,1:T(8,128)(2,1)} copy(bf16[512,2048]{1,0:T(8,128)(2,1)} %param.5) | data formatting | bytes 4194304 | tf_op args[1]
  82.6 3.9 %copy.11 = bf16[512,16,128]{2,0,1:T(8,128)(2,1)} copy(bf16[512,16,128]{0,2,1:T(8,128)(2,1)} %bitcast.42) | data formatting | bytes 4194304 | tf_op jit(solution)/shard_map/reshape | solution.py:282
  86.5 35.4 %all-to-all-done.3 = f32[16,64,640]{2,1,0:T(8,128)S(1)} async-done(((f32[16,64,640]{2,1,0:T(8,128)}), f32[16,64,640]{2,1,0:T(8,128)S(1)}, u32[]{:S(2)}, u32[]{:S(2)}) %all-to-all-start.3) | async-done | bytes 2621472 | tf_op jit(solution)/shard_map/all_to_all | solution.py:256
  121.9 0.0 all-gather.4.cloned.1.call-update
  122.0 0.0 copy-start.4
  122.0 4.5 %all-to-all-start.4 = ((bf16[16,512,128]{2,1,0:T(8,128)(2,1)}), bf16[16,512,128]{2,1,0:T(8,128)(2,1)}, u32[]{:S(2)}, u32[]{:S(2)}) async-start(bf16[16,512,128]{2,1,0:T(8,128)(2,1)} %bitcast.41), calls=%async_computation.4 | async-start | bytes 4194304 | tf_op jit(solution)/shard_map/all_to_all | solution.py:284
  126.4 0.0 copy-done.4
  126.5 0.1 fusion.18
  126.5 0.2 convert_reduce_fusion
  126.7 0.1 select_reduce_fusion
  126.8 0.1 pad_add_fusion.order_ref
  126.9 62.4 %shard_map.59 = (f32[1024,1024]{1,0:T(8,128)S(1)}, f32[512,128]{1,0:T(8,128)S(1)}) custom-call(s32[8]{0:T(128)S(1)} %pad_add_fusion.order_ref, s32[1]{0:T(128)} %bitcast.18.own_ref, f32[1024,640]{1,0:T(8,128)S(1)} %bitcast.39), custom_call_target="tpu_custom_call" | custom-call | tf_op jit(solution)/shard_map/pallas_call | solution.py:194
  189.3 0.0 copy-start
  189.3 2.0 copy-done
  191.3 0.0 all-to-all-done.4.trail_ref
  191.3 0.0 all-gather.6.cloned.1.call-done
  191.3 0.0 copy-start.1
  191.3 2.2 copy-done.1
  193.5 13.9 %shard_map.60 = f32[1024,128]{1,0:T(8,128)} custom-call(bf16[16,1024,512]{2,1,0:T(8,128)(2,1)} %bitcast.40, bf16[16,512,128]{2,1,0:T(8,128)(2,1)} %all-to-all-done.4.trail_ref, f32[1024,1024]{1,0:T(8,128)S(1)} %copy-done.1), custom_call_target="tpu_custom_call" | custom-call | tf_op jit(solution)/shard_map/pallas_call | solution.py:235
  207.4 9.5 %all-to-all-start.5 = ((f32[16,64,128]{2,1,0:T(8,128)}), f32[16,64,128]{2,1,0:T(8,128)S(1)}, u32[]{:S(2)}, u32[]{:S(2)}) async-start(f32[16,64,128]{2,1,0:T(8,128)} %bitcast.20), calls=%async_computation.5 | async-start | bytes 1048576 | tf_op jit(solution)/shard_map/all_to_all | solution.py:290
  216.9 0.6 fusion.17
  220.1 0.0 copy-start.3
  220.1 8.4 %all-gather.4.cloned.1.call-done = f32[1024,1024]{1,0:T(8,128)} async-done(((f32[64,1024]{1,0:T(8,128)}), f32[1024,1024]{1,0:T(8,128)}) %all-gather.4.cloned.1.call-update) | async-done | bytes 4194320 | tf_op jit(solution)/shard_map/all_gather | solution.py:285
  228.5 1.7 constant_dynamic-slice_fusion.3
  230.1 0.0 copy-done.3
  230.1 2.2 fusion.8
  232.4 3.5 %all-to-all-done.5 = f32[16,64,128]{2,1,0:T(8,128)S(1)} async-done(((f32[16,64,128]{2,1,0:T(8,128)}), f32[16,64,128]{2,1,0:T(8,128)S(1)}, u32[]{:S(2)}, u32[]{:S(2)}) %all-to-all-start.5) | async-done | bytes 524320 | tf_op jit(solution)/shard_map/all_to_all | solution.py:290
  235.9 0.8 copy_bitcast_fusion
  (3 shorter events, 0.1 us)
Async XLA Ops:
  7.2 20.7 %copy-start.2 = (bf16[512,64]{0,1:T(8,128)(2,1)S(1)}, bf16[512,64]{0,1:T(8,128)(2,1)}, u32[]{:S(2)}) copy-start(bf16[512,64]{0,1:T(8,128)(2,1)} %param.4) | copy-start | bytes 196612
  7.2 184.1 %all-gather.6.cloned.1.call-start = ((), (), s32[]{:S(2)}) async-start(), calls=%async_computation.7 | async-start | bytes 16842752 | tf_op jit(solution)/shard_map/all_gather | solution.py:271
  54.5 17.8 %all-to-all-start.2 = ((f32[16,8,512]{2,1,0:T(8,128)}), f32[16,8,512]{2,1,0:T(8,128)S(1)}, u32[]{:S(2)}, u32[]{:S(2)}) async-start(f32[16,8,512]{2,1,0:T(8,128)} %broadcast_in_dim.13), calls=%async_computation.2 | async-start | bytes 524288 | tf_op jit(solution)/shard_map/all_to_all | solution.py:256
  74.1 47.8 %all-to-all-start.3 = ((f32[16,64,640]{2,1,0:T(8,128)}), f32[16,64,640]{2,1,0:T(8,128)S(1)}, u32[]{:S(2)}, u32[]{:S(2)}) async-start(f32[16,64,640]{2,1,0:T(8,128)} %broadcast_in_dim.14), calls=%async_computation.3 | async-start | bytes 5242880 | tf_op jit(solution)/shard_map/all_to_all | solution.py:256
  78.6 149.9 %all-gather.4.cloned.1.call-start = ((), (), s32[]{:S(2)}) async-start(), calls=%async_computation.6 | async-start | bytes 4456448 | tf_op jit(solution)/shard_map/all_gather | solution.py:285
  122.0 4.5 %copy-start.4 = (s32[8]{0:T(128)S(1)}, s32[8]{0:T(128)}, u32[]{:S(2)}) copy-start(s32[8]{0:T(128)} %param.7) | copy-start | bytes 100
  122.0 69.3 %all-to-all-start.4 = ((bf16[16,512,128]{2,1,0:T(8,128)(2,1)}), bf16[16,512,128]{2,1,0:T(8,128)(2,1)}, u32[]{:S(2)}, u32[]{:S(2)}) async-start(bf16[16,512,128]{2,1,0:T(8,128)(2,1)} %bitcast.41), calls=%async_computation.4 | async-start | bytes 4194304 | tf_op jit(solution)/shard_map/all_to_all | solution.py:284
  189.3 2.0 copy-start
  191.3 2.2 copy-start.1
  207.4 28.5 %all-to-all-start.5 = ((f32[16,64,128]{2,1,0:T(8,128)}), f32[16,64,128]{2,1,0:T(8,128)S(1)}, u32[]{:S(2)}, u32[]{:S(2)}) async-start(f32[16,64,128]{2,1,0:T(8,128)} %bitcast.20), calls=%async_computation.5 | async-start | bytes 1048576 | tf_op jit(solution)/shard_map/all_to_all | solution.py:290
  220.1 10.1 %copy-start.3 = (f32[1024,64]{0,1:T(8,128)S(1)}, f32[1024,64]{0,1:T(8,128)}, u32[]{:S(2)}) copy-start(f32[1024,64]{0,1:T(8,128)} %param.6) | copy-start | bytes 786436
Sparse Core Ops, SparseCore 0:
  11.6 174.0 all-gather.5
  187.6 40.8 all-gather.3

commit v4 on v3

--- a/solution.py
+++ b/solution.py
@@ -289,6 +289,7 @@
     solved = slab_call(everything.reshape(n_row, 1024, span), trail, inverse_factor, tokens)
     slab_rows = lax.all_to_all(solved.reshape(n_row, 1024 // n_row, -1), "row", 0, 0)
     slab_factor = slab_rows.transpose(1, 0, 2).reshape(1024 // n_row, -1)
+    slab_factor, weight_all = lax.optimization_barrier((slab_factor, weight_all))
     pruned = jnp.concatenate(
         [lax.dynamic_slice_in_dim(weight_all, block_order[q] * NB, NB, 0) for q in range(4)], 0
     )

time: 244 us -> 248 us (1.016)
  waiting for transfers between devices: 62.3 us -> 66.3 us
    all_to_all x1, waiting for transfers between devices: 3.51 us -> 15.9 us  [on_device(): lax.all_to_all(solved.reshape(n_row, 1024 // n_row, -1), 'row', 0, 0)]
    all_gather x1, waiting for transfers between devices: 8.41 us -> 0.01 us  [on_device(): weight_all = lax.all_gather(weight_in, 'col', axis=0, tiled=True)]
  transfers between devices with their start and end apart: 6 -> 6, of which waited for: 4 -> 3; matrix products, arithmetic and copies ran while one was open for 7% -> 6% of each run, Pallas kernels for 31% -> 31%
where the time goes in v4:
time: 248 us; the launch traced here: 247 us
  Pallas kernels  76 us (31%)
  waiting for transfers between devices  66.3 us (27%)
  blocking collectives  44.4 us (18%)
  starting transfers between devices  22.1 us (9%)
  local copies, waits for them, and re-layouts  18.7 us (8%)
  between operations  16.7 us (7%)
  matrix products  2.67 us (1%)
    pallas_call x1, Pallas kernels, factor_call(): pl.pallas_call(functools.partial(kernel, tokens), out_shape=(jax.ShapeDty...  62.1 us
    all_to_all x2, waiting for transfers between devices, spread(): return lax.all_to_all(jnp.broadcast_to(x[None], (n,) + x.shape), axis, 0, 0)  49.6 us
    all_to_all x1, blocking collectives, on_device(): piece = lax.all_to_all(pieces, 'row', 0, 0).sum(0)  25.5 us
    all_to_all x1, blocking collectives, spread(): return lax.all_to_all(jnp.broadcast_to(x[None], (n,) + x.shape), axis, 0, 0)  19 us
    all_to_all x1, waiting for transfers between devices, on_device(): lax.all_to_all(solved.reshape(n_row, 1024 // n_row, -1), 'row', 0, 0)  15.9 us
    pallas_call x1, Pallas kernels, slab_call(): pl.pallas_call(functools.partial(slab_kernel, tokens), grid=(groups // ea...  13.9 us
    all_to_all x1, starting transfers between devices, on_device(): lax.all_to_all(solved.reshape(n_row, 1024 // n_row, -1), 'row', 0, 0)  9.48 us
    unnamed x11, local copies, waits for them, and re-layouts  8.13 us
  transfers between devices with their start and end apart: 6, of which 3 were waited for; matrix products, arithmetic and copies ran while one was open for 6% of the time, Pallas kernels for 31%

profile of v4, /device:TPU:2, one launch (start us, length us, event | category | flops | bytes accessed | tf_op | source)
XLA Modules:
  0.0 247.3 jit_solution(10372078427271440046)
XLA Ops:
  7.2 0.0 copy-start.2
  7.2 0.0 all-gather.6.cloned.1.call-start
  7.2 0.7 all-gather.6.cloned.1.call-update
  7.9 0.9 broadcast_in_dim.12
  8.8 19.0 %all_to_all.30 = bf16[16,64,512]{2,1,0:T(8,128)(2,1)S(1)} all-to-all(bf16[16,64,512]{2,1,0:T(8,128)(2,1)S(1)} %broadcast_in_dim.12), channel_id=1, replica_groups=mesh['row'=16,'col'=16] {'col'}, dimensions={0} | all-to-all | bytes 2097152 | tf_op jit(solution)/shard_map/all_to_all | solution.py:256
  27.8 0.0 copy-done.2
  27.8 0.4 fusion.13
  28.3 25.5 %all_to_all.31 = f32[16,8,512]{2,1,0:T(8,128)S(1)} all-to-all(f32[16,8,512]{2,1,0:T(8,128)S(1)} %bitcast.46), channel_id=1, replica_groups=mesh['row'=16,'col'=16] {'row'}, dimensions={0} | all-to-all | bytes 524288 | tf_op jit(solution)/shard_map/all_to_all | solution.py:275
  53.8 0.7 broadcast_in_dim.13
  54.5 3.5 %all-to-all-start.2 = ((f32[16,8,512]{2,1,0:T(8,128)}), f32[16,8,512]{2,1,0:T(8,128)S(1)}, u32[]{:S(2)}, u32[]{:S(2)}) async-start(f32[16,8,512]{2,1,0:T(8,128)} %broadcast_in_dim.13), calls=%async_computation.2 | async-start | bytes 524288 | tf_op jit(solution)/shard_map/all_to_all | solution.py:256
  58.0 14.2 %all-to-all-done.2 = f32[16,8,512]{2,1,0:T(8,128)S(1)} async-done(((f32[16,8,512]{2,1,0:T(8,128)}), f32[16,8,512]{2,1,0:T(8,128)S(1)}, u32[]{:S(2)}, u32[]{:S(2)}) %all-to-all-start.2) | async-done | bytes 262176 | tf_op jit(solution)/shard_map/all_to_all | solution.py:256
  72.3 1.8 broadcast_in_dim.14
  74.1 4.5 %all-to-all-start.3 = ((f32[16,64,640]{2,1,0:T(8,128)}), f32[16,64,640]{2,1,0:T(8,128)S(1)}, u32[]{:S(2)}, u32[]{:S(2)}) async-start(f32[16,64,640]{2,1,0:T(8,128)} %broadcast_in_dim.14), calls=%async_computation.3 | async-start | bytes 5242880 | tf_op jit(solution)/shard_map/all_to_all | solution.py:256
  78.6 0.0 all-gather.4.cloned.1.call-start
  78.6 4.0 %copy.10 = bf16[512,2048]{0,1:T(8,128)(2,1)} copy(bf16[512,2048]{1,0:T(8,128)(2,1)} %param.5) | data formatting | bytes 4194304 | tf_op args[1]
  82.6 3.9 %copy.11 = bf16[512,16,128]{2,0,1:T(8,128)(2,1)} copy(bf16[512,16,128]{0,2,1:T(8,128)(2,1)} %bitcast.42) | data formatting | bytes 4194304 | tf_op jit(solution)/shard_map/reshape | solution.py:282
  86.5 35.4 %all-to-all-done.3 = f32[16,64,640]{2,1,0:T(8,128)S(1)} async-done(((f32[16,64,640]{2,1,0:T(8,128)}), f32[16,64,640]{2,1,0:T(8,128)S(1)}, u32[]{:S(2)}, u32[]{:S(2)}) %all-to-all-start.3) | async-done | bytes 2621472 | tf_op jit(solution)/shard_map/all_to_all | solution.py:256
  121.9 0.0 all-gather.4.cloned.1.call-update
  122.0 0.0 copy-start.4
  122.0 4.5 %all-to-all-start.4 = ((bf16[16,512,128]{2,1,0:T(8,128)(2,1)}), bf16[16,512,128]{2,1,0:T(8,128)(2,1)}, u32[]{:S(2)}, u32[]{:S(2)}) async-start(bf16[16,512,128]{2,1,0:T(8,128)(2,1)} %bitcast.41), calls=%async_computation.4 | async-start | bytes 4194304 | tf_op jit(solution)/shard_map/all_to_all | solution.py:284
  126.4 0.0 copy-done.4
  126.5 0.1 fusion.18
  126.5 0.2 convert_reduce_fusion
  126.7 0.1 select_reduce_fusion
  126.8 0.1 pad_add_fusion.order_ref
  126.9 62.1 %shard_map.59 = (f32[1024,1024]{1,0:T(8,128)S(1)}, f32[512,128]{1,0:T(8,128)S(1)}) custom-call(s32[8]{0:T(128)S(1)} %pad_add_fusion.order_ref, s32[1]{0:T(128)} %bitcast.18.own_ref, f32[1024,640]{1,0:T(8,128)S(1)} %bitcast.39), custom_call_target="tpu_custom_call" | custom-call | tf_op jit(solution)/shard_map/pallas_call | solution.py:194
  189.0 0.0 copy-start
  189.0 2.0 copy-done
  191.0 0.0 all-to-all-done.4.trail_ref
  191.0 0.0 all-gather.6.cloned.1.call-done
  191.0 0.0 copy-start.1
  191.0 2.2 copy-done.1
  193.2 13.9 %shard_map.60 = f32[1024,128]{1,0:T(8,128)} custom-call(bf16[16,1024,512]{2,1,0:T(8,128)(2,1)} %bitcast.40, bf16[16,512,128]{2,1,0:T(8,128)(2,1)} %all-to-all-done.4.trail_ref, f32[1024,1024]{1,0:T(8,128)S(1)} %copy-done.1), custom_call_target="tpu_custom_call" | custom-call | tf_op jit(solution)/shard_map/pallas_call | solution.py:235
  207.1 9.5 %all-to-all-start.5 = ((f32[16,64,128]{2,1,0:T(8,128)}), f32[16,64,128]{2,1,0:T(8,128)S(1)}, u32[]{:S(2)}, u32[]{:S(2)}) async-start(f32[16,64,128]{2,1,0:T(8,128)} %bitcast.20), calls=%async_computation.5 | async-start | bytes 1048576 | tf_op jit(solution)/shard_map/all_to_all | solution.py:290
  216.6 0.6 fusion.17
  219.7 15.9 %all-to-all-done.5 = f32[16,64,128]{2,1,0:T(8,128)S(1)} async-done(((f32[16,64,128]{2,1,0:T(8,128)}), f32[16,64,128]{2,1,0:T(8,128)S(1)}, u32[]{:S(2)}, u32[]{:S(2)}) %all-to-all-start.5) | async-done | bytes 524320 | tf_op jit(solution)/shard_map/all_to_all | solution.py:290
  235.7 0.8 copy_bitcast_fusion
  236.5 0.0 copy-start.3
  236.5 0.0 all-gather.4.cloned.1.call-done
  236.5 1.7 constant_dynamic-slice_fusion.3
  238.2 0.0 copy-done.3
  238.2 2.2 fusion.8
  (3 shorter events, 0.1 us)
Async XLA Ops:
  7.2 20.7 %copy-start.2 = (bf16[512,64]{0,1:T(8,128)(2,1)S(1)}, bf16[512,64]{0,1:T(8,128)(2,1)}, u32[]{:S(2)}) copy-start(bf16[512,64]{0,1:T(8,128)(2,1)} %param.4) | copy-start | bytes 196612
  7.2 183.8 %all-gather.6.cloned.1.call-start = ((), (), s32[]{:S(2)}) async-start(), calls=%async_computation.7 | async-start | bytes 16842752 | tf_op jit(solution)/shard_map/all_gather | solution.py:271
  54.5 17.8 %all-to-all-start.2 = ((f32[16,8,512]{2,1,0:T(8,128)}), f32[16,8,512]{2,1,0:T(8,128)S(1)}, u32[]{:S(2)}, u32[]{:S(2)}) async-start(f32[16,8,512]{2,1,0:T(8,128)} %broadcast_in_dim.13), calls=%async_computation.2 | async-start | bytes 524288 | tf_op jit(solution)/shard_map/all_to_all | solution.py:256
  74.1 47.8 %all-to-all-start.3 = ((f32[16,64,640]{2,1,0:T(8,128)}), f32[16,64,640]{2,1,0:T(8,128)S(1)}, u32[]{:S(2)}, u32[]{:S(2)}) async-start(f32[16,64,640]{2,1,0:T(8,128)} %broadcast_in_dim.14), calls=%async_computation.3 | async-start | bytes 5242880 | tf_op jit(solution)/shard_map/all_to_all | solution.py:256
  78.6 157.9 %all-gather.4.cloned.1.call-start = ((), (), s32[]{:S(2)}) async-start(), calls=%async_computation.6 | async-start | bytes 4456448 | tf_op jit(solution)/shard_map/all_gather | solution.py:285
  122.0 4.5 %copy-start.4 = (s32[8]{0:T(128)S(1)}, s32[8]{0:T(128)}, u32[]{:S(2)}) copy-start(s32[8]{0:T(128)} %param.7) | copy-start | bytes 100
  122.0 69.0 %all-to-all-start.4 = ((bf16[16,512,128]{2,1,0:T(8,128)(2,1)}), bf16[16,512,128]{2,1,0:T(8,128)(2,1)}, u32[]{:S(2)}, u32[]{:S(2)}) async-start(bf16[16,512,128]{2,1,0:T(8,128)(2,1)} %bitcast.41), calls=%async_computation.4 | async-start | bytes 4194304 | tf_op jit(solution)/shard_map/all_to_all | solution.py:284
  189.0 2.0 copy-start
  191.0 2.2 copy-start.1
  207.1 28.6 %all-to-all-start.5 = ((f32[16,64,128]{2,1,0:T(8,128)}), f32[16,64,128]{2,1,0:T(8,128)S(1)}, u32[]{:S(2)}, u32[]{:S(2)}) async-start(f32[16,64,128]{2,1,0:T(8,128)} %bitcast.20), calls=%async_computation.5 | async-start | bytes 1048576 | tf_op jit(solution)/shard_map/all_to_all | solution.py:290
  236.5 1.7 copy-start.3
Sparse Core Ops, SparseCore 0:
  11.6 174.0 all-gather.5
  187.6 40.2 all-gather.3
